TPU v7x, 256 devices: a whole 4x4x8 slice. The times are simulated.
256 devices in a mesh: enc: 4 (over z_lo), seq: 64 (over x, z_hi, y, core).
Axes of the slice: x: 4, y: 4, z: 8 (z_hi: 2, z_lo: 4; z = z_hi * 4 + z_lo), core: 2. Of those that a mesh axis runs over, the one named last changes fastest.
Arguments:
- q_proj: bfloat16 [64, 512, 3072], P('seq', 'enc')
- k_proj: bfloat16 [64, 512, 3072], P('seq', 'enc')
- v_proj: bfloat16 [64, 512, 3072], P('seq', 'enc'), may hold values from -6 to 6
- residual_in: bfloat16 [64, 512, 3072], P('seq', 'enc'), may hold values from -6 to 6
- upstream: bfloat16 [64, 512, 3072], P('seq', 'enc'), may hold values from -3 to 3
- enc_hidden: bfloat16 [64, 512, 1536], P('seq', 'enc')
- enc_gain: float32 [1536], replicated, may hold values from 0.5 to 1.5
- enc_bias: float32 [1536], replicated, may hold values from -3 to 3
- proj_weight: bfloat16 [3072, 1536], P(('enc', 'seq')), may hold values from -0.109375 to 0.109375
- patch_map: int32 [64, 512], P('seq', 'enc'), may hold values from 0 to 511, each once within a row
Outputs:
- d_query: bfloat16 [64, 512, 3072], P('seq', 'enc')
- d_key: bfloat16 [64, 512, 3072], P('seq', 'enc')
- d_value: bfloat16 [64, 512, 3072], P('seq', 'enc')
- d_residual: bfloat16 [64, 512, 3072], P('seq', 'enc')
- w_grad: float32 [3072, 1536], P(('enc', 'seq'))
Inputs may be any that keep to these rules, and one draw needn't show every extreme that they name: `patch_map`: each frame's row names every one of the frame's 512 encoder patches exactly once.
All inputs are finite; a program needn't handle non-finite values.
Results may differ from a plain program's by a relative error of at most 0.034.
Values may be sent and summed in bfloat16 or wider, within the bound.
A program may use at most 128 MiB of HBM per device.

v0:
```python
import jax
import jax.numpy as jnp
from jax import lax
from jax.sharding import PartitionSpec as P

HEAD_DIM = 128


align_coef = 128.0
epsilon = 1e-06


def norm_rows(states, gain_vec, bias_vec):
    values_f = states.astype(jnp.float32)
    row_mean = jnp.mean(values_f, axis=-1, keepdims=True)
    row_var = jnp.mean((values_f - row_mean) ** 2, axis=-1, keepdims=True)
    return ((values_f - row_mean) * lax.rsqrt(row_var + epsilon) * gain_vec + bias_vec).astype(
        jnp.bfloat16
    )


def split_heads(array_in):
    frame_count, token_count, feature_width = array_in.shape
    return array_in.reshape(frame_count, token_count, feature_width // HEAD_DIM, HEAD_DIM)


def attend_forward(queries, keys_in, values_in, residual):
    attn_scale = HEAD_DIM ** (-0.5)
    scores = (
        jnp.einsum(
            "fqhd,fkhd->fhqk",
            split_heads(queries),
            split_heads(keys_in),
            preferred_element_type=jnp.float32,
        )
        * attn_scale
    )
    row_max = jnp.max(scores, axis=-1, keepdims=True)
    expo = jnp.exp(scores - row_max)
    attn_probs = expo / jnp.sum(expo, axis=-1, keepdims=True)
    probs_low = attn_probs.astype(jnp.bfloat16)
    attn_out = jnp.einsum(
        "fhqk,fkhd->fqhd", probs_low, split_heads(values_in), preferred_element_type=jnp.float32
    )
    attn_out = attn_out.astype(jnp.bfloat16).reshape(queries.shape)
    hidden = (residual.astype(jnp.float32) + attn_out.astype(jnp.float32)).astype(jnp.bfloat16)
    return (attn_probs, probs_low, attn_out, hidden)


def attend_backward(attn_probs, probs_low, attn_out, d_out, queries, keys_in, values_in):
    attn_scale = HEAD_DIM ** (-0.5)
    grad_heads = split_heads(d_out)
    d_value = jnp.einsum(
        "fhqk,fqhd->fkhd", probs_low, grad_heads, preferred_element_type=jnp.float32
    ).astype(jnp.bfloat16)
    d_probs = jnp.einsum(
        "fqhd,fkhd->fhqk", grad_heads, split_heads(values_in), preferred_element_type=jnp.float32
    )
    row_dot = jnp.sum(
        grad_heads.astype(jnp.float32) * split_heads(attn_out).astype(jnp.float32), axis=-1
    )
    row_dot = jnp.transpose(row_dot, (0, 2, 1))[..., None]
    d_scores = (attn_probs * (d_probs - row_dot) * attn_scale).astype(jnp.bfloat16)
    d_query = jnp.einsum(
        "fhqk,fkhd->fqhd", d_scores, split_heads(keys_in), preferred_element_type=jnp.float32
    ).astype(jnp.bfloat16)
    d_key = jnp.einsum(
        "fhqk,fqhd->fkhd", d_scores, split_heads(queries), preferred_element_type=jnp.float32
    ).astype(jnp.bfloat16)
    return (
        d_query.reshape(queries.shape),
        d_key.reshape(queries.shape),
        d_value.reshape(queries.shape),
    )


def align_grad(z_proj, targets):
    target_f32 = targets.astype(jnp.float32)
    norm_z = jnp.sqrt(jnp.sum(z_proj * z_proj, axis=-1, keepdims=True) + epsilon)
    norm_y = jnp.sqrt(jnp.sum(target_f32 * target_f32, axis=-1, keepdims=True) + epsilon)
    cosine = jnp.sum(z_proj * target_f32, axis=-1, keepdims=True) / (norm_z * norm_y)
    return (
        -align_coef * (target_f32 / (norm_z * norm_y) - cosine * z_proj / (norm_z * norm_z))
    ).astype(jnp.bfloat16)


def per_device(
    q_proj,
    k_proj,
    v_proj,
    residual_in,
    upstream,
    enc_hidden,
    enc_gain,
    enc_bias,
    proj_weight,
    patch_map,
):
    weight_rows = lax.all_gather(proj_weight, "seq", axis=0, tiled=True)
    targets_src = norm_rows(enc_hidden, enc_gain, enc_bias)
    frame_feats = lax.all_gather(targets_src, "enc", axis=1, tiled=True)
    queries, keys_in, values_in, residual = (
        lax.all_to_all(q_proj, "enc", split_axis=2, concat_axis=1, tiled=True),
        lax.all_to_all(k_proj, "enc", split_axis=2, concat_axis=1, tiled=True),
        lax.all_to_all(v_proj, "enc", split_axis=2, concat_axis=1, tiled=True),
        lax.all_to_all(residual_in, "enc", split_axis=2, concat_axis=1, tiled=True),
    )
    attn_probs, probs_low, attn_out, hidden = attend_forward(queries, keys_in, values_in, residual)
    flipped = jnp.swapaxes(hidden, 0, 1)
    z_own = jnp.swapaxes(
        lax.psum_scatter(
            jnp.einsum("tfd,de->tfe", flipped, weight_rows, preferred_element_type=jnp.float32),
            "enc",
            scatter_dimension=0,
            tiled=True,
        ),
        0,
        1,
    )
    targets = jnp.take_along_axis(frame_feats, patch_map[:, :, None], axis=1)
    d_own = align_grad(z_own, targets)
    d_align = lax.all_gather(d_own, "enc", axis=1, tiled=True)
    d_above = lax.all_to_all(upstream, "enc", split_axis=2, concat_axis=1, tiled=True)
    d_back = jnp.einsum("fte,de->ftd", d_align, weight_rows, preferred_element_type=jnp.float32)
    d_hidden = (d_above.astype(jnp.float32) + d_back).astype(jnp.bfloat16)
    w_local = jnp.einsum("ftd,fte->de", hidden, d_align, preferred_element_type=jnp.float32)
    w_grad = lax.psum_scatter(w_local, "seq", scatter_dimension=0, tiled=True)
    d_query, d_key, d_value = attend_backward(
        attn_probs, probs_low, attn_out, d_hidden, queries, keys_in, values_in
    )
    out_query, out_key, out_value, out_residual = (
        lax.all_to_all(d_query, "enc", split_axis=1, concat_axis=2, tiled=True),
        lax.all_to_all(d_key, "enc", split_axis=1, concat_axis=2, tiled=True),
        lax.all_to_all(d_value, "enc", split_axis=1, concat_axis=2, tiled=True),
        lax.all_to_all(d_hidden, "enc", split_axis=1, concat_axis=2, tiled=True),
    )
    return (out_query, out_key, out_value, out_residual, w_grad)


def solution(mesh):
    in_specs = (
        P("seq", "enc", None),
        P("seq", "enc", None),
        P("seq", "enc", None),
        P("seq", "enc", None),
        P("seq", "enc", None),
        P("seq", "enc", None),
        P(),
        P(),
        P(("enc", "seq"), None),
        P("seq", "enc"),
    )
    out_specs = (
        P("seq", "enc", None),
        P("seq", "enc", None),
        P("seq", "enc", None),
        P("seq", "enc", None),
        P(("enc", "seq"), None),
    )
    return jax.shard_map(
        per_device, mesh=mesh, in_specs=in_specs, out_specs=out_specs, check_vma=False
    )
```

profile of v0, /device:TPU:34, one launch (start us, length us, event | category | flops | bytes accessed | tf_op | source)
XLA Modules:
  0.0 774.2 jit_solution(4964337419854751033)
XLA Ops:
  7.9 3.7 copy.107
  12.2 17.0 %reduce.14 = bf16[3072,128]{1,0:T(8,128)(2,1)S(1)} reduce(bf16[3072,1,128]{2,1,0:T(2,128)(2,1)S(1)} %bitcast.180, bf16[]{:T(256)} %broadcast.237), dimensions={1}, to_apply=%bitcast.142.reduce_sub_computation | reduce | bytes 1572866
  30.2 6.1 all-to-all-start
  38.2 17.0 %reduce.10 = bf16[3072,128]{1,0:T(8,128)(2,1)S(1)} reduce(bf16[3072,1,128]{2,1,0:T(2,128)(2,1)S(1)} %bitcast.193, bf16[]{:T(256)} %broadcast.237), dimensions={1}, to_apply=%bitcast.144.reduce_sub_computation | reduce | bytes 1572866
  56.2 7.4 all-to-all-start.1
  65.6 17.0 %reduce.12 = bf16[3072,128]{1,0:T(8,128)(2,1)S(1)} reduce(bf16[3072,1,128]{2,1,0:T(2,128)(2,1)S(1)} %bitcast.194, bf16[]{:T(256)} %broadcast.237), dimensions={1}, to_apply=%bitcast.138.reduce_sub_computation | reduce | bytes 1572866
  83.6 4.1 all-to-all-done.1
  87.6 9.7 %all-to-all-start.3 = ((bf16[4,2,49152]{2,1,0:T(2,128)(2,1)}), bf16[4,2,49152]{2,1,0:T(2,128)(2,1)S(1)}, u32[]{:S(2)}, u32[]{:S(2)}) async-start(bf16[4,2,49152]{2,1,0:T(2,128)(2,1)} %reshape.516), calls=%async_computation.3 | async-start | bytes 1572864 | tf_op jit(solution)/shard_map/all_to_all | solution.py:106
  99.3 17.1 %reduce.13 = bf16[3072,128]{1,0:T(8,128)(2,1)S(1)} reduce(bf16[3072,1,128]{2,1,0:T(2,128)(2,1)S(1)} %bitcast.195, bf16[]{:T(256)} %broadcast.237), dimensions={1}, to_apply=%bitcast.140.reduce_sub_computation | reduce | bytes 1572866
  117.5 5.1 all-to-all-start.4
  124.2 2.4 reshape.517
  128.4 2.8 reshape.521
  133.1 2.4 reshape.523
  138.4 2.5 reshape.519
  142.8 2.2 copy.116
  144.9 4.8 fusion.38
  149.7 3.8 fusion.6
  156.6 4.9 reshape.512
  161.4 5.0 convolution_bitcast_fusion
  168.3 3.0 gather_fusion
  171.2 66.3 %reduce-scatter.4.cloned.1.call-done = f32[128,1,1536]{2,0,1:T(8,128)} async-done(((f32[512,1,1536]{2,0,1:T(8,128)}), f32[128,1,1536]{2,0,1:T(8,128)}) %reduce-scatter.4.cloned.1.call-update) | async-done | bytes 786448 | tf_op jit(solution)/shard_map/reduce_scatter | solution.py:111
  240.8 4.4 copy.113
  245.1 18.9 %reduce.11 = bf16[3072,128]{1,0:T(8,128)(2,1)} reduce(bf16[3072,1,128]{2,1,0:T(2,128)(2,1)} %bitcast.196, bf16[]{:T(256)} %broadcast.237), dimensions={1}, to_apply=%bitcast.136.reduce_sub_computation | reduce | bytes 1572866
  266.0 32.6 %all_to_all.135 = bf16[4,2,49152]{2,1,0:T(2,128)(2,1)} all-to-all(bf16[4,2,49152]{2,1,0:T(2,128)(2,1)} %reshape.514), channel_id=1, replica_groups=mesh['enc'=4,'seq'=64] {'enc'}, dimensions={0} | all-to-all | bytes 1572864 | tf_op jit(solution)/shard_map/all_to_all | solution.py:123
  298.7 3.8 reshape.515
  302.5 4.2 bitcast_convert_fusion.1
  306.6 3.1 copy.114
  309.7 4.9 fusion.8
  314.6 2.3 copy.120
  316.9 3.2 convolution_convert_fusion.2
  320.1 3.7 copy.132
  323.8 5.5 reduce.17
  330.3 6.3 all-to-all-start.7
  336.9 2.4 copy.165
  339.3 7.4 reduce.18
  349.2 4.4 all-to-all-done.7
  353.7 7.8 %all-to-all-start.8 = ((bf16[4,2,49152]{2,1,0:T(2,128)(2,1)}), bf16[4,2,49152]{2,1,0:T(2,128)(2,1)}, u32[]{:S(2)}, u32[]{:S(2)}) async-start(bf16[4,2,49152]{2,1,0:T(2,128)(2,1)} %reshape.530), calls=%async_computation.9 | async-start | bytes 1572864 | tf_op jit(solution)/shard_map/all_to_all | solution.py:135
  361.5 4.1 multiply_convert_fusion
  367.7 3.7 copy.129
  371.4 6.3 reduce.16
  379.7 6.2 all-to-all-start.6
  387.6 3.6 fusion.13
  393.4 5.5 reduce.15
  400.7 3.5 fusion.9
  404.2 5.1 all-to-all-start.5
  409.3 213.8 %fusion = f32[16,1536]{1,0:T(8,128)S(1)} fusion(f32[768,1536]{1,0:T(8,128)} %fusion.9), kind=kCustom, calls=%all-reduce-scatter | all-reduce-scatter fusion | flops 1572865 | bytes 4817920
  623.1 4.5 collective-permute-start.15
  629.6 17.3 %collective-permute-start.13 = (f32[16,1536]{1,0:T(8,128)S(1)}, f32[16,1536]{1,0:T(8,128)S(1)}, u32[]{:S(2)}, u32[]{:S(2)}) collective-permute-start(f32[16,1536]{1,0:T(8,128)S(1)} %fusion), channel_id=1, source_target_pairs={{0,14},{1,15},{2,16},{3,17},{4,18},{5,19},{6,20},{7,21},{8,22},{9,... | collective-permute-start | bytes 294920
  650.7 4.7 collective-permute-done.15
  657.4 12.3 %collective-permute-start.9 = (f32[16,1536]{1,0:T(8,128)S(1)}, f32[16,1536]{1,0:T(8,128)S(1)}, u32[]{:S(2)}, u32[]{:S(2)}) collective-permute-start(f32[16,1536]{1,0:T(8,128)S(1)} %fusion), channel_id=1, source_target_pairs={{0,10},{1,11},{2,12},{3,13},{4,14},{5,15},{6,16},{7,17},{8,18},{9,... | collective-permute-start | bytes 294920
  669.7 3.4 collective-permute-start.8
  673.2 4.2 collective-permute-start.7
  677.4 2.9 collective-permute-start.6
  680.4 14.5 %collective-permute-start.5 = (f32[16,1536]{1,0:T(8,128)S(1)}, f32[16,1536]{1,0:T(8,128)S(1)}, u32[]{:S(2)}, u32[]{:S(2)}) collective-permute-start(f32[16,1536]{1,0:T(8,128)S(1)} %fusion), channel_id=1, source_target_pairs={{0,6},{1,7},{2,8},{3,9},{4,10},{5,11},{6,12},{7,13},{8,14},{9,15},... | collective-permute-start | bytes 294920
  696.8 4.0 collective-permute-start.3
  700.8 8.0 %collective-permute-start.2 = (f32[16,1536]{1,0:T(8,128)S(1)}, f32[16,1536]{1,0:T(8,128)S(1)}, u32[]{:S(2)}, u32[]{:S(2)}) collective-permute-start(f32[16,1536]{1,0:T(8,128)S(1)} %fusion), channel_id=1, source_target_pairs={{0,3},{1,4},{2,5},{3,6},{4,7},{5,8},{6,9},{7,10},{8,11},{9,12},{10... | collective-permute-start | bytes 294920
  708.8 4.3 collective-permute-start.1
  713.1 2.8 collective-permute-start
  717.2 5.0 collective-permute-done.1
  722.2 3.8 collective-permute-done
  726.0 25.2 %concatenate = f32[268,1536]{1,0:T(8,128)} concatenate(f32[12,1536]{1,0:T(8,128)S(1)} %collective-permute-done.15, f32[16,1536]{1,0:T(8,128)S(1)} %collective-permute-done.14, f32[16,1536]{1,0:T(8,128)S(1)} %collective-permute-done.13, f32[16,1536]{1,0:T(8,128)S(1)} %collective-permute-done.12, f32[16,1536]{1,0:T(8,128)S(1)} %collective-permute-done.11, ...), dimensions={0} | concatenate | bytes 3293184
  752.7 2.4 reshape.529
  756.8 2.4 reshape.531
  760.9 2.4 reshape.527
  (149 shorter events, 63.4 us)
Async XLA Ops:
  7.2 149.4 %all-gather.9.cloned.1.call-start = ((), (), s32[]{:S(2)}) async-start(), calls=%async_computation.13 | async-start | bytes 3194880 | tf_op jit(solution)/shard_map/all_gather | solution.py:99
  30.2 6.1 copy-start.19
  30.2 26.0 %all-to-all-start = ((bf16[4,2,49152]{2,1,0:T(2,128)(2,1)}), bf16[4,2,49152]{2,1,0:T(2,128)(2,1)S(1)}, u32[]{:S(2)}, u32[]{:S(2)}) async-start(bf16[4,2,49152]{2,1,0:T(2,128)(2,1)} %reshape.520), calls=%async_computation | async-start | bytes 1572864 | tf_op jit(solution)/shard_map/all_to_all | solution.py:103
  56.2 7.4 copy-start.20
  56.2 9.3 %copy-start.15 = (bf16[4,2,49152]{2,1,0:T(2,128)(2,1)}, bf16[4,2,49152]{2,1,0:T(2,128)(2,1)S(1)}, u32[]{:S(2)}) copy-start(bf16[4,2,49152]{2,1,0:T(2,128)(2,1)S(1)} %all-to-all-done) | copy-start | bytes 2359300
  56.2 31.4 %all-to-all-start.1 = ((bf16[4,2,49152]{2,1,0:T(2,128)(2,1)}), bf16[4,2,49152]{2,1,0:T(2,128)(2,1)}, u32[]{:S(2)}, u32[]{:S(2)}) async-start(bf16[4,2,49152]{2,1,0:T(2,128)(2,1)} %reshape.522), calls=%async_computation.1 | async-start | bytes 1572864 | tf_op jit(solution)/shard_map/all_to_all | solution.py:104
  83.6 13.8 %copy-start.21 = (bf16[1,128,3072]{2,1,0:T(8,128)(2,1)S(1)}, bf16[1,128,3072]{2,1,0:T(8,128)(2,1)}, u32[]{:S(2)}) copy-start(bf16[1,128,3072]{2,1,0:T(8,128)(2,1)} %param.12) | copy-start | bytes 2359300
  87.6 29.8 %all-to-all-start.3 = ((bf16[4,2,49152]{2,1,0:T(2,128)(2,1)}), bf16[4,2,49152]{2,1,0:T(2,128)(2,1)S(1)}, u32[]{:S(2)}, u32[]{:S(2)}) async-start(bf16[4,2,49152]{2,1,0:T(2,128)(2,1)} %reshape.516), calls=%async_computation.3 | async-start | bytes 1572864 | tf_op jit(solution)/shard_map/all_to_all | solution.py:106
  99.3 18.1 %copy-start.8 = (bf16[1,128,1536]{2,1,0:T(8,128)(2,1)S(1)}, bf16[1,128,1536]{2,1,0:T(8,128)(2,1)}, u32[]{:S(2)}) copy-start(bf16[1,128,1536]{2,1,0:T(8,128)(2,1)} %param.15) | copy-start | bytes 1179652
  117.3 5.5 copy-start.23
  117.3 5.5 copy-start.24
  117.5 6.5 copy-start.16
  117.5 20.9 %all-to-all-start.4 = ((bf16[4,2,49152]{2,1,0:T(2,128)(2,1)}), bf16[4,2,49152]{2,1,0:T(2,128)(2,1)}, u32[]{:S(2)}, u32[]{:S(2)}) async-start(bf16[4,2,49152]{2,1,0:T(2,128)(2,1)} %reshape.518), calls=%async_computation.4 | async-start | bytes 1572864 | tf_op jit(solution)/shard_map/all_to_all | solution.py:105
  122.6 45.7 %all-gather.5.cloned.1.call-start = ((), (), s32[]{:S(2)}) async-start(), calls=%async_computation.10 | async-start | bytes 1966080 | tf_op jit(solution)/shard_map/all_gather | solution.py:101
  124.0 113.5 %reduce-scatter.4.cloned.1.call-start = ((), (), s32[]{:S(2)}) async-start(), calls=%async_computation.11 | async-start | bytes 3932160 | tf_op jit(solution)/shard_map/reduce_scatter | solution.py:111
  128.4 14.4 %copy-start.2 = (f32[1,128,3072]{1,0,2:T(1,128)}, f32[1,128,3072]{1,0,2:T(1,128)S(1)}, u32[]{:S(2)}) copy-start(f32[1,128,3072]{1,0,2:T(1,128)S(1)} %bitcast_convert_fusion) | copy-start | bytes 4718596
  142.8 2.2 copy-start.9
  142.8 2.2 copy-start.11
  149.7 3.8 copy-start.17
  153.5 1.8 copy-start.7
  154.1 1.2 copy-start
  166.5 0.7 copy-start.27
  166.5 143.2 %all-gather.7.cloned.1.call-start = ((), (), s32[]{:S(2)}) async-start(), calls=%async_computation.12 | async-start | bytes 1966080 | tf_op jit(solution)/shard_map/all_gather | solution.py:122
  237.5 1.6 copy-start.14
  329.3 7.3 copy-start.6
  330.3 23.4 %all-to-all-start.7 = ((bf16[4,2,49152]{2,1,0:T(2,128)(2,1)}), bf16[4,2,49152]{2,1,0:T(2,128)(2,1)}, u32[]{:S(2)}, u32[]{:S(2)}) async-start(bf16[4,2,49152]{2,1,0:T(2,128)(2,1)} %reshape.528), calls=%async_computation.8 | async-start | bytes 1572864 | tf_op jit(solution)/shard_map/all_to_all | solution.py:134
  339.3 9.5 %copy-start.1 = (f32[6,512,128]{1,2,0:T(8,128)S(1)}, f32[6,512,128]{1,2,0:T(8,128)}, u32[]{:S(2)}) copy-start(f32[6,512,128]{1,2,0:T(8,128)} %copy-done) | copy-start | bytes 4718596
  349.2 12.3 %copy-start.13 = (bf16[512,768]{0,1:T(8,128)(2,1)S(1)}, bf16[512,768]{0,1:T(8,128)(2,1)}, u32[]{:S(2)}) copy-start(bf16[512,768]{0,1:T(8,128)(2,1)} %copy.120) | copy-start | bytes 2359300
  349.2 12.3 %copy-start.18 = (bf16[512,6,128]{0,2,1:T(8,128)(2,1)S(1)}, bf16[512,6,128]{0,2,1:T(8,128)(2,1)}, u32[]{:S(2)}) copy-start(bf16[512,6,128]{0,2,1:T(8,128)(2,1)} %reshape.484) | copy-start | bytes 2359300
  353.7 26.0 %all-to-all-start.8 = ((bf16[4,2,49152]{2,1,0:T(2,128)(2,1)}), bf16[4,2,49152]{2,1,0:T(2,128)(2,1)}, u32[]{:S(2)}, u32[]{:S(2)}) async-start(bf16[4,2,49152]{2,1,0:T(2,128)(2,1)} %reshape.530), calls=%async_computation.9 | async-start | bytes 1572864 | tf_op jit(solution)/shard_map/all_to_all | solution.py:135
  361.5 4.1 copy-start.12
  365.6 2.0 copy-start.4
  379.7 24.5 %all-to-all-start.6 = ((bf16[4,2,49152]{2,1,0:T(2,128)(2,1)}), bf16[4,2,49152]{2,1,0:T(2,128)(2,1)}, u32[]{:S(2)}, u32[]{:S(2)}) async-start(bf16[4,2,49152]{2,1,0:T(2,128)(2,1)} %reshape.526), calls=%async_computation.7 | async-start | bytes 1572864 | tf_op jit(solution)/shard_map/all_to_all | solution.py:133
  385.9 1.7 copy-start.3
  387.6 3.6 copy-start.5
  387.6 3.6 copy-start.10
  393.4 6.6 copy-start.22
  399.0 1.7 copy-start.26
  404.2 360.9 %all-to-all-start.5 = ((bf16[4,2,49152]{2,1,0:T(2,128)(2,1)}), bf16[4,2,49152]{2,1,0:T(2,128)(2,1)S(1)}, u32[]{:S(2)}, u32[]{:S(2)}) async-start(bf16[4,2,49152]{2,1,0:T(2,128)(2,1)} %reshape.524), calls=%async_computation.6 | async-start | bytes 1572864 | tf_op jit(solution)/shard_map/all_to_all | solution.py:132
  409.3 306.6 %copy-start.25 = (u32[256]{0:T(256)S(1)}, u32[256]{0:T(256)}, u32[]{:S(2)}) copy-start(u32[256]{0:T(256)} %constant.40) | copy-start | bytes 3076
  623.1 32.4 %collective-permute-start.15 = (f32[12,1536]{1,0:T(8,128)S(1)}, f32[12,1536]{1,0:T(8,128)S(1)}, u32[]{:S(2)}, u32[]{:S(2)}) collective-permute-start(f32[12,1536]{1,0:T(8,128)S(1)} %slice.2), channel_id=1, source_target_pairs={{0,16},{1,17},{2,18},{3,19},{4,20},{5,21},{6,22},{7,23},{8,24},{9,... | collective-permute-start | bytes 221192
  627.7 29.7 %collective-permute-start.14 = (f32[16,1536]{1,0:T(8,128)S(1)}, f32[16,1536]{1,0:T(8,128)S(1)}, u32[]{:S(2)}, u32[]{:S(2)}) collective-permute-start(f32[16,1536]{1,0:T(8,128)S(1)} %fusion), channel_id=1, source_target_pairs={{0,15},{1,16},{2,17},{3,18},{4,19},{5,20},{6,21},{7,22},{8,23},{9,... | collective-permute-start | bytes 294920
  629.6 40.2 %collective-permute-start.13 = (f32[16,1536]{1,0:T(8,128)S(1)}, f32[16,1536]{1,0:T(8,128)S(1)}, u32[]{:S(2)}, u32[]{:S(2)}) collective-permute-start(f32[16,1536]{1,0:T(8,128)S(1)} %fusion), channel_id=1, source_target_pairs={{0,14},{1,15},{2,16},{3,17},{4,18},{5,19},{6,20},{7,21},{8,22},{9,... | collective-permute-start | bytes 294920
  646.9 26.3 %collective-permute-start.12 = (f32[16,1536]{1,0:T(8,128)S(1)}, f32[16,1536]{1,0:T(8,128)S(1)}, u32[]{:S(2)}, u32[]{:S(2)}) collective-permute-start(f32[16,1536]{1,0:T(8,128)S(1)} %fusion), channel_id=1, source_target_pairs={{0,13},{1,14},{2,15},{3,16},{4,17},{5,18},{6,19},{7,20},{8,21},{9,... | collective-permute-start | bytes 294920
  648.8 28.6 %collective-permute-start.11 = (f32[16,1536]{1,0:T(8,128)S(1)}, f32[16,1536]{1,0:T(8,128)S(1)}, u32[]{:S(2)}, u32[]{:S(2)}) collective-permute-start(f32[16,1536]{1,0:T(8,128)S(1)} %fusion), channel_id=1, source_target_pairs={{0,12},{1,13},{2,14},{3,15},{4,16},{5,17},{6,18},{7,19},{8,20},{9,... | collective-permute-start | bytes 294920
  655.5 24.9 %collective-permute-start.10 = (f32[16,1536]{1,0:T(8,128)S(1)}, f32[16,1536]{1,0:T(8,128)S(1)}, u32[]{:S(2)}, u32[]{:S(2)}) collective-permute-start(f32[16,1536]{1,0:T(8,128)S(1)} %fusion), channel_id=1, source_target_pairs={{0,11},{1,12},{2,13},{3,14},{4,15},{5,16},{6,17},{7,18},{8,19},{9,... | collective-permute-start | bytes 294920
  657.4 37.5 %collective-permute-start.9 = (f32[16,1536]{1,0:T(8,128)S(1)}, f32[16,1536]{1,0:T(8,128)S(1)}, u32[]{:S(2)}, u32[]{:S(2)}) collective-permute-start(f32[16,1536]{1,0:T(8,128)S(1)} %fusion), channel_id=1, source_target_pairs={{0,10},{1,11},{2,12},{3,13},{4,14},{5,15},{6,16},{7,17},{8,18},{9,... | collective-permute-start | bytes 294920
  669.7 27.1 %collective-permute-start.8 = (f32[16,1536]{1,0:T(8,128)S(1)}, f32[16,1536]{1,0:T(8,128)S(1)}, u32[]{:S(2)}, u32[]{:S(2)}) collective-permute-start(f32[16,1536]{1,0:T(8,128)S(1)} %fusion), channel_id=1, source_target_pairs={{0,9},{1,10},{2,11},{3,12},{4,13},{5,14},{6,15},{7,16},{8,17},{9,1... | collective-permute-start | bytes 294920
  673.2 27.6 %collective-permute-start.7 = (f32[16,1536]{1,0:T(8,128)S(1)}, f32[16,1536]{1,0:T(8,128)S(1)}, u32[]{:S(2)}, u32[]{:S(2)}) collective-permute-start(f32[16,1536]{1,0:T(8,128)S(1)} %fusion), channel_id=1, source_target_pairs={{0,8},{1,9},{2,10},{3,11},{4,12},{5,13},{6,14},{7,15},{8,16},{9,17... | collective-permute-start | bytes 294920
  677.4 31.4 %collective-permute-start.6 = (f32[16,1536]{1,0:T(8,128)S(1)}, f32[16,1536]{1,0:T(8,128)S(1)}, u32[]{:S(2)}, u32[]{:S(2)}) collective-permute-start(f32[16,1536]{1,0:T(8,128)S(1)} %fusion), channel_id=1, source_target_pairs={{0,7},{1,8},{2,9},{3,10},{4,11},{5,12},{6,13},{7,14},{8,15},{9,16}... | collective-permute-start | bytes 294920
  680.4 32.7 %collective-permute-start.5 = (f32[16,1536]{1,0:T(8,128)S(1)}, f32[16,1536]{1,0:T(8,128)S(1)}, u32[]{:S(2)}, u32[]{:S(2)}) collective-permute-start(f32[16,1536]{1,0:T(8,128)S(1)} %fusion), channel_id=1, source_target_pairs={{0,6},{1,7},{2,8},{3,9},{4,10},{5,11},{6,12},{7,13},{8,14},{9,15},... | collective-permute-start | bytes 294920
  694.9 22.3 %collective-permute-start.4 = (f32[16,1536]{1,0:T(8,128)S(1)}, f32[16,1536]{1,0:T(8,128)S(1)}, u32[]{:S(2)}, u32[]{:S(2)}) collective-permute-start(f32[16,1536]{1,0:T(8,128)S(1)} %fusion), channel_id=1, source_target_pairs={{0,5},{1,6},{2,7},{3,8},{4,9},{5,10},{6,11},{7,12},{8,13},{9,14},{... | collective-permute-start | bytes 294920
  696.8 20.4 %collective-permute-start.3 = (f32[16,1536]{1,0:T(8,128)S(1)}, f32[16,1536]{1,0:T(8,128)S(1)}, u32[]{:S(2)}, u32[]{:S(2)}) collective-permute-start(f32[16,1536]{1,0:T(8,128)S(1)} %fusion), channel_id=1, source_target_pairs={{0,4},{1,5},{2,6},{3,7},{4,8},{5,9},{6,10},{7,11},{8,12},{9,13},{1... | collective-permute-start | bytes 294920
  700.8 16.4 %collective-permute-start.2 = (f32[16,1536]{1,0:T(8,128)S(1)}, f32[16,1536]{1,0:T(8,128)S(1)}, u32[]{:S(2)}, u32[]{:S(2)}) collective-permute-start(f32[16,1536]{1,0:T(8,128)S(1)} %fusion), channel_id=1, source_target_pairs={{0,3},{1,4},{2,5},{3,6},{4,7},{5,8},{6,9},{7,10},{8,11},{9,12},{10... | collective-permute-start | bytes 294920
  708.8 13.4 %collective-permute-start.1 = (f32[16,1536]{1,0:T(8,128)S(1)}, f32[16,1536]{1,0:T(8,128)S(1)}, u32[]{:S(2)}, u32[]{:S(2)}) collective-permute-start(f32[16,1536]{1,0:T(8,128)S(1)} %fusion), channel_id=1, source_target_pairs={{0,2},{1,3},{2,4},{3,5},{4,6},{5,7},{6,8},{7,9},{8,10},{9,11},{10,... | collective-permute-start | bytes 294920
  713.1 12.9 %collective-permute-start = (f32[16,1536]{1,0:T(8,128)S(1)}, f32[16,1536]{1,0:T(8,128)S(1)}, u32[]{:S(2)}, u32[]{:S(2)}) collective-permute-start(f32[16,1536]{1,0:T(8,128)S(1)} %fusion), channel_id=1, source_target_pairs={{0,1},{1,2},{2,3},{3,4},{4,5},{5,6},{6,7},{7,8},{8,9},{9,10},{10,1... | collective-permute-start | bytes 294920
Sparse Core Ops, SparseCore 0:
  11.6 86.6 all-gather.8
  125.2 42.2 all-gather.4
  170.1 67.3 reduce-scatter.3
  240.9 53.1 all-gather.6
where the time goes:
time: 785 us; the launch traced here: 774 us
  blocking collectives  246 us (31%)
  starting transfers between devices  142 us (18%)
  other arithmetic  133 us (17%)
  local copies, waits for them, and re-layouts  119 us (15%)
  waiting for transfers between devices  90 us (11%)
  matrix products  28.6 us (4%)
  between operations  15.4 us (2%)
    unnamed x1, blocking collectives  214 us
    unnamed x9, other arithmetic  112 us
    unnamed x96, local copies, waits for them, and re-layouts  88 us
    unnamed x16, starting transfers between devices  87.8 us
    reduce_scatter x1, waiting for transfers between devices, per_device(): lax.psum_scatter(jnp.einsum('tfd,de->tfe', flipped, weight_rows, preferre...  66.3 us
    all_to_all x1, blocking collectives, per_device(): lax.all_to_all(upstream, 'enc', split_axis=2, concat_axis=1, tiled=True)  32.6 us
  transfers between devices with their start and end apart: 28, of which 7 were waited for; matrix products, arithmetic and copies ran while one was open for 60% of the time, Pallas kernels for 0%

commit v1 on v0

v1 whole, which is shorter than its diff:
```python
import math

import jax
import jax.numpy as jnp
from jax import lax
from jax.experimental import pallas as pl
from jax.experimental.pallas import tpu as pltpu
from jax.sharding import PartitionSpec as P

HD = 128
D = 3072
E = 1536
FT = 512
TOK = 128
HW = 768
PW = 256
QUARTER = 384
NX, NY, NZH, NE = 4, 4, 2, 4
ALIGN = 128.0
EPS = 1e-6
SCALE = HD**-0.5
SCALE2 = SCALE * math.log2(math.e)
BF = jnp.bfloat16
F32 = jnp.float32
NT = (((1,), (1,)), ((), ()))
NN = (((1,), (0,)), ((), ()))


def mm(a, b, dims=NN):
    return lax.dot_general(a, b, dims, preferred_element_type=F32)


SCRATCH = {
    "encv": ((TOK, E), BF),
    "qh": ((FT, HW), BF),
    "kh": ((FT, HW), BF),
    "vh": ((FT, HW), BF),
    "pt": ((6, FT, FT), BF),
    "ob": ((FT, HW), BF),
    "oh": ((2 * TOK, E), BF),
    "rh": ((2 * TOK, E), BF),
    "uh": ((2 * TOK, E), BF),
    "hid": ((2 * TOK, E), BF),
    "hidt": ((E, 2 * TOK), BF),
    "za": ((2 * TOK, E), F32),
    "zr": ((TOK, E), F32),
    "ts": ((TOK, E), BF),
    "tsl": ((FT, QUARTER), BF),
    "tpm": ((FT, QUARTER), BF),
    "tg": ((TOK, E), BF),
    "pmb": ((NE, 8, 128), jnp.int32),
    "pmo": ((8, 128), jnp.int32),
    "wy": ((2, NZH, NY, 32, E), BF),
    "wh": ((E, E), BF),
    "dzb": ((2 * TOK, E), BF),
    "drs": ((2 * TOK, E), BF),
    "doh": ((FT, HW), BF),
    "dqb": ((FT, HW), BF),
    "dkb": ((FT, HW), BF),
    "dvb": ((FT, HW), BF),
    "gb": ((2, NX, 192, E), BF),
    "gt": ((2, 192, E), BF),
    "gl": ((4, 192, E), BF),
    "gy": ((2, NZH, NY, 32, E), BF),
    "yt": ((2, NZH, 32, E), BF),
    "yl": ((4, NZH, 32, E), BF),
    "gz": ((8, 16, E), BF),
}
NSEM = 400


def kernel(
    q, k, v, res, ups, enc, gain, bias, wpad, pm, dq, dk, dv, dres, wg, *scratch
):
    r = dict(zip(SCRATCH, scratch[: len(SCRATCH)], strict=True))
    sem = scratch[len(SCRATCH)]
    top = [0]

    def sems(n):
        base = top[0]
        top[0] += n
        assert top[0] <= NSEM
        return base

    e = lax.axis_index("enc")
    s = lax.axis_index("seq")
    c = lax.rem(s, 2)
    y = lax.rem(s // 2, NY)
    zh = lax.rem(s // 8, NZH)
    x = s // 16
    o = 1 - c

    def seq_of(xx, zz, yy, cc):
        return ((xx * NZH + zz) * NY + yy) * 2 + cc

    def dev(ee=None, xx=None, zz=None, yy=None, cc=None):
        return (
            e if ee is None else ee,
            seq_of(
                x if xx is None else xx,
                zh if zz is None else zz,
                y if yy is None else yy,
                c if cc is None else cc,
            ),
        )

    sibling = dev(cc=o)
    pending = []

    def put(src, dst, rs, target, here=None):
        ss = sems(1)
        copy = pltpu.make_async_remote_copy(
            src_ref=src,
            dst_ref=dst,
            send_sem=sem.at[ss],
            recv_sem=sem.at[rs],
            device_id=target,
            device_id_type=pl.DeviceIdType.MESH,
        )
        if here is None:
            copy.start()
            pending.append((None, copy))
            return
        away = jnp.logical_not(here)

        @pl.when(here)
        def _():
            pltpu.make_async_copy(src, dst, sem.at[rs]).start()

        @pl.when(away)
        def _():
            copy.start()

        pending.append((away, copy))

    def local(src, dst, rs):
        pltpu.make_async_copy(src, dst, sem.at[rs]).start()

    def wait(dst, rs):
        pltpu.make_async_copy(dst, dst, sem.at[rs]).wait()

    def col(start, width):
        return pl.ds(pl.multiple_of(start, 128), width)

    def row(start, width):
        return pl.ds(pl.multiple_of(start, 16), width)

    barrier = pltpu.get_barrier_semaphore()
    mine = (zh * NE + e) * 2 + c
    greeted = []
    for n in range(1, 16):
        other = lax.rem(mine + n, 16)
        greeted.append(
            dev(ee=lax.rem(other // 2, NE), zz=other // 8, cc=lax.rem(other, 2))
        )
    for step in (1, 3):
        greeted.append(dev(yy=lax.rem(y + step, NY)))
        greeted.append(dev(xx=lax.rem(x + step, NX)))

    enc_sem = sems(1)
    local(enc.at[0], r["encv"], enc_sem)
    qkv_sem = sems(3 * 3 * NE)
    qkv = ((q, r["qh"]), (k, r["kh"]), (v, r["vh"]))
    for p in range(3):
        for a, (src, dst) in enumerate(qkv):
            local(
                src.at[0, :, col(e * HW + p * PW, PW)],
                dst.at[row(e * TOK, TOK), pl.ds(p * PW, PW)],
                qkv_sem + (p * 3 + a) * NE + e,
            )
    half_sem = sems(4)
    local(res.at[0, :, col(c * E, E)], r["rh"].at[row(c * TOK, TOK)], half_sem)
    local(ups.at[0, :, col(c * E, E)], r["uh"].at[row(c * TOK, TOK)], half_sem + 1)

    for target in greeted:
        pl.semaphore_signal(
            barrier, inc=1, device_id=target, device_id_type=pl.DeviceIdType.MESH
        )
    pl.semaphore_wait(barrier, len(greeted))

    half = e // 2
    side = lax.rem(e, 2)
    w_sem = sems(8)
    for n in range(8):
        other = lax.rem(zh * NE + e + n, 8)
        put(
            wpad,
            r["wy"].at[side, zh, y, row(c * 16, 16)],
            w_sem + (side * NZH + zh) * 2 + c,
            dev(ee=lax.rem(other, NE), zz=other // NE, cc=half),
            (half == c) if n == 0 else None,
        )

    def send_qkv(p):
        for n in range(1, NE):
            j = lax.rem(e + n, NE)
            for a, (src, dst) in enumerate(qkv):
                put(
                    src.at[0, :, col(j * HW + p * PW, PW)],
                    dst.at[row(e * TOK, TOK), pl.ds(p * PW, PW)],
                    qkv_sem + (p * 3 + a) * NE + e,
                    dev(ee=j),
                )

    def wait_qkv(p):
        for a, (_, dst) in enumerate(qkv):
            for j in range(NE):
                wait(
                    dst.at[pl.ds(j * TOK, TOK), pl.ds(p * PW, PW)],
                    qkv_sem + (p * 3 + a) * NE + j,
                )

    send_qkv(0)
    put(
        res.at[0, :, col(o * E, E)],
        r["rh"].at[row(c * TOK, TOK)],
        half_sem + 2,
        sibling,
    )
    put(
        ups.at[0, :, col(o * E, E)],
        r["uh"].at[row(c * TOK, TOK)],
        half_sem + 3,
        sibling,
    )

    wait(r["encv"], enc_sem)
    r["pmo"][...] = jnp.broadcast_to(pm[...], (8, 128))

    def norm(i, _):
        rows = row(i * 32, 32)
        t = r["encv"][rows, :].astype(F32)
        mean = jnp.mean(t, axis=-1, keepdims=True)
        t = t - mean
        var = jnp.mean(t * t, axis=-1, keepdims=True)
        r["ts"][rows, :] = (t * lax.rsqrt(var + EPS) * gain[...] + bias[...]).astype(BF)
        return 0

    lax.fori_loop(0, TOK // 32, norm, 0)
    t_sem, pm_sem = sems(NE), sems(NE)
    for n in range(NE):
        j = lax.rem(e + n, NE)
        src = r["ts"].at[:, col(j * QUARTER, QUARTER)]
        dst = r["tsl"].at[row(e * TOK, TOK)]
        if n:
            put(src, dst, t_sem + e, dev(ee=j))
            put(r["pmo"], r["pmb"].at[e], pm_sem + e, dev(ee=j))
        else:
            local(src, dst, t_sem + e)
            local(r["pmo"], r["pmb"].at[e], pm_sem + e)
    send_qkv(1)
    send_qkv(2)

    class Gather:
        def __init__(self, m, to, piece):
            self.m, self.to, self.piece = m, to, piece
            self.sem = sems(6)
            self.up, self.down = lax.rem(m + 1, 4), lax.rem(m + 3, 4)

        def start(self):
            for i in range(2):
                own = self.piece(self.m, i)
                put(own, own, self.sem + i, self.to(self.up))
                put(own, own, self.sem + 2 + i, self.to(self.down))

        def forward(self):
            first = self.piece(self.down, 0)
            wait(first, self.sem)
            put(first, first, self.sem + 4, self.to(self.up))
            second = self.piece(self.up, 1)
            wait(second, self.sem + 3)
            put(second, second, self.sem + 5, self.to(self.down))

        def finish(self):
            wait(self.piece(self.down, 1), self.sem + 1)
            wait(self.piece(self.up, 0), self.sem + 2)
            far = lax.rem(self.m + 2, 4)
            wait(self.piece(far, 0), self.sem + 4)
            wait(self.piece(far, 1), self.sem + 5)

    for i in range(2):
        for zz in range(NZH):
            for cc in range(2):
                wait(
                    r["wy"].at[i, zz, y, pl.ds(cc * 16, 16)],
                    w_sem + (i * NZH + zz) * 2 + cc,
                )
    gather_y = Gather(
        y, lambda m: dev(yy=m), lambda m, i: r["wy"].at[i, :, m]
    )
    gather_y.start()
    gather_y.forward()
    gather_y.finish()
    ri = lax.broadcasted_iota(jnp.int32, (96, 128), 0)
    ci = lax.broadcasted_iota(jnp.int32, (96, 128), 1)
    keep = jnp.logical_and((ci >> 4) * 12 + (ci & 15) == ri, (ci & 15) < 12)
    squeeze = jnp.where(keep, 1.0, 0.0).astype(BF)
    for i in range(2):
        for zz in range(NZH):
            block = r["wy"][i, zz].reshape(128, E)
            r["wh"][row(i * HW + x * 192 + zz * 96, 96), :] = mm(squeeze, block).astype(
                BF
            )
    gather_x = Gather(
        x,
        lambda m: dev(xx=m),
        lambda m, i: r["wh"].at[row(i * HW + m * 192, 192)],
    )
    gather_x.start()

    o_sem = sems(3 * 4)

    def forward(p):
        wait_qkv(p)

        def head(hh, _):
            h = p * 2 + hh
            cols = col(h * HD, HD)
            kk = r["kh"][:, cols]
            vt = jnp.transpose(r["vh"][:, cols])
            for t in range(2):
                rows = pl.ds(t * 256, 256)
                sc = mm(kk, r["qh"][rows, cols], NT)
                ex = jnp.exp2((sc - jnp.max(sc, axis=0, keepdims=True)) * SCALE2)
                pr = (ex * (1.0 / jnp.sum(ex, axis=0, keepdims=True))).astype(BF)
                r["pt"][h, :, rows] = pr
                r["ob"][rows, cols] = jnp.transpose(mm(vt, pr)).astype(BF)
            return 0

        lax.fori_loop(0, 2, head, 0)
        for n in range(NE):
            j = lax.rem(e + n, NE)
            put(
                r["ob"].at[row(j * TOK, TOK), pl.ds(p * PW, PW)],
                r["oh"].at[row(c * TOK, TOK), col(side * HW + p * PW, PW)],
                o_sem + p * 4 + c * 2 + side,
                dev(ee=j, cc=half),
                (half == c) if n == 0 else None,
            )

    forward(0)

    tb_sem = sems(NE)
    for j in range(NE):
        wait(r["tsl"].at[pl.ds(j * TOK, TOK)], t_sem + j)
        wait(r["pmb"].at[j], pm_sem + j)

    def permute(j, _):
        names = r["pmb"][j][0:1, :]
        at = lax.broadcasted_iota(jnp.int32, (FT, TOK), 0)
        pick = jnp.where(at == names, 1.0, 0.0)
        pick = jnp.transpose(pick).astype(BF)
        r["tpm"][row(j * TOK, TOK), :] = mm(pick, r["tsl"][...]).astype(BF)
        return 0

    lax.fori_loop(0, NE, permute, 0)
    for n in range(NE):
        j = lax.rem(e + n, NE)
        src = r["tpm"].at[row(j * TOK, TOK)]
        dst = r["tg"].at[:, col(e * QUARTER, QUARTER)]
        if n:
            put(src, dst, tb_sem + e, dev(ee=j))
        else:
            local(src, dst, tb_sem + e)

    forward(1)
    gather_x.forward()
    forward(2)
    gather_x.finish()

    for n in range(4):
        wait(r["rh" if n % 2 == 0 else "uh"].at[row((c if n < 2 else o) * TOK, TOK)], half_sem + n)

    def hidden(p):
        for i in range(2):
            cols = pl.ds(i * HW + p * PW, PW)
            for f in range(2):
                wait(r["oh"].at[pl.ds(f * TOK, TOK), cols], o_sem + p * 4 + f * 2 + i)
            r["hid"][:, cols] = (
                r["rh"][:, cols].astype(F32) + r["oh"][:, cols].astype(F32)
            ).astype(BF)

    def project(p, rows):
        part = 0.0
        for i in range(2):
            cols = pl.ds(i * HW + p * PW, PW)
            part = part + mm(r["hid"][rows, cols], r["wh"][cols, :])
        return part

    every = pl.ds(0, 2 * TOK)
    hidden(0)
    r["za"][...] = project(0, every)
    hidden(1)
    r["za"][...] += project(1, every)
    hidden(2)
    theirs, ours = row(o * TOK, TOK), row(c * TOK, TOK)
    z_sem = sems(1)
    r["za"][theirs, :] += project(2, theirs)
    put(r["za"].at[theirs], r["zr"], z_sem, sibling)
    r["za"][ours, :] += project(2, ours)
    for j in range(NE):
        wait(r["tg"].at[:, pl.ds(j * QUARTER, QUARTER)], tb_sem + j)
    wait(r["zr"], z_sem)

    def align(i, _):
        rows = row(i * 32, 32)
        z = r["za"][row(c * TOK + i * 32, 32), :] + r["zr"][rows, :]
        t = r["tg"][rows, :].astype(F32)
        nz = jnp.sqrt(jnp.sum(z * z, axis=-1, keepdims=True) + EPS)
        ny = jnp.sqrt(jnp.sum(t * t, axis=-1, keepdims=True) + EPS)
        cosine = jnp.sum(z * t, axis=-1, keepdims=True) / (nz * ny)
        r["dzb"][row(c * TOK + i * 32, 32), :] = (
            -ALIGN * (t * (1.0 / (nz * ny)) - z * (cosine / (nz * nz)))
        ).astype(BF)
        return 0

    lax.fori_loop(0, TOK // 32, align, 0)
    dz_sem = sems(1)
    put(r["dzb"].at[ours], r["dzb"].at[ours], dz_sem, sibling)
    wait(r["dzb"].at[theirs], dz_sem)

    do_sem, dr_sem = sems(3 * NE), sems(2 * 6)
    for p in range(3):
        for i in range(2):
            cols = pl.ds(i * HW + p * PW, PW)
            back = mm(r["dzb"][...], r["wh"][cols, :], NT)
            r["drs"][:, cols] = (r["uh"][:, cols].astype(F32) + back).astype(BF)
            for f in (c, o):
                put(
                    r["drs"].at[row(f * TOK, TOK), cols],
                    r["doh"].at[row(e * TOK, TOK), pl.ds(p * PW, PW)],
                    do_sem + p * NE + e,
                    dev(ee=c * 2 + i, cc=f),
                    (c * 2 + i == e) if f is c else None,
                )
    for p in range(3):
        for i in range(2):
            cols = pl.ds(i * HW + p * PW, PW)
            out = dres.at[0, :, col(c * E + i * HW + p * PW, PW)]
            local(r["drs"].at[ours, cols], out, dr_sem + p * 2 + i)
            put(r["drs"].at[theirs, cols], out, dr_sem + 6 + p * 2 + i, sibling)

    def transpose(i, _):
        cols = col(i * 256, 256)
        r["hidt"][row(i * 256, 256), :] = jnp.transpose(r["hid"][:, cols])
        return 0

    lax.fori_loop(0, 6, transpose, 0)

    def partial(m, i):
        a = r["hidt"][row(i * HW + m * 192, 192), :]

        def tile(n, _):
            cols = col(n * 512, 512)
            r["gb"][i, m, :, cols] = mm(a, r["dzb"][:, cols]).astype(BF)
            return 0

        lax.fori_loop(0, 3, tile, 0)

    class Scatter:
        def __init__(self, m, to, piece, transit, arrive):
            self.m, self.to, self.piece = m, to, piece
            self.transit, self.arrive = transit, arrive
            self.sem = sems(6)
            self.up, self.down = lax.rem(m + 1, 4), lax.rem(m + 3, 4)
            self.far = lax.rem(m + 2, 4)

        def start_far(self):
            put(self.piece(self.far, 0), self.transit(0), self.sem, self.to(self.up))
            put(self.piece(self.far, 1), self.transit(1), self.sem + 1, self.to(self.down))

        def start_near(self):
            put(self.piece(self.up, 1), self.arrive(1), self.sem + 3, self.to(self.up))
            put(self.piece(self.down, 0), self.arrive(2), self.sem + 4, self.to(self.down))

        def add(self, into, *others):
            def step(n, _):
                at = into.at[..., col(n * 512, 512)]
                total = at[...].astype(F32)
                for other in others:
                    total += other[..., col(n * 512, 512)].astype(F32)
                at[...] = total.astype(BF)
                return 0

            lax.fori_loop(0, 3, step, 0)

        def forward(self):
            wait(self.transit(0), self.sem)
            self.add(self.piece(self.up, 0), self.transit(0))
            put(self.piece(self.up, 0), self.arrive(0), self.sem + 2, self.to(self.up))
            wait(self.transit(1), self.sem + 1)
            self.add(self.piece(self.down, 1), self.transit(1))
            put(self.piece(self.down, 1), self.arrive(3), self.sem + 5, self.to(self.down))

        def finish(self):
            for n in range(4):
                wait(self.arrive(n), self.sem + 2 + n)
            self.add(self.piece(self.m, 0), self.arrive(0), self.arrive(2))
            self.add(self.piece(self.m, 1), self.arrive(1), self.arrive(3))

    scatter_x = Scatter(
        x,
        lambda m: dev(xx=m),
        lambda m, i: r["gb"].at[i, m],
        lambda i: r["gt"].at[i],
        lambda n: r["gl"].at[n],
    )
    scatter_y = Scatter(
        y,
        lambda m: dev(yy=m),
        lambda m, i: r["gy"].at[i, :, m],
        lambda i: r["yt"].at[i],
        lambda n: r["yl"].at[n],
    )
    for i in range(2):
        partial(scatter_x.far, i)
    scatter_x.start_far()
    partial(scatter_x.up, 1)
    partial(scatter_x.down, 0)
    scatter_x.start_near()
    partial(scatter_x.up, 0)
    partial(scatter_x.down, 1)
    for i in range(2):
        partial(x, i)

    out_sem = sems(3 * 3 * NE)
    grads = ((r["dqb"], dq), (r["dkb"], dk), (r["dvb"], dv))

    def backward(p):
        for j in range(NE):
            wait(
                r["doh"].at[pl.ds(j * TOK, TOK), pl.ds(p * PW, PW)],
                do_sem + p * NE + j,
            )

        def head(hh, _):
            h = p * 2 + hh
            cols = col(h * HD, HD)
            vv = r["vh"][:, cols]
            kt = jnp.transpose(r["kh"][:, cols])
            gv = gk = 0.0
            for t in range(2):
                rows = pl.ds(t * 256, 256)
                go = r["doh"][rows, cols]
                dp = mm(vv, go, NT)
                low = r["pt"][h, :, rows]
                pr = low.astype(F32)
                dot = jnp.sum(pr * dp, axis=0, keepdims=True)
                ds = (pr * (dp - dot) * SCALE).astype(BF)
                gv = gv + mm(low, go)
                gk = gk + mm(ds, r["qh"][rows, cols])
                r["dqb"][rows, cols] = jnp.transpose(mm(kt, ds)).astype(BF)
            r["dvb"][:, cols] = gv.astype(BF)
            r["dkb"][:, cols] = gk.astype(BF)
            return 0

        lax.fori_loop(0, 2, head, 0)
        for n in range(NE):
            j = lax.rem(e + n, NE)
            for a, (src, dst) in enumerate(grads):
                here = src.at[row(j * TOK, TOK), pl.ds(p * PW, PW)]
                there = dst.at[0, :, col(e * HW + p * PW, PW)]
                rs = out_sem + (p * 3 + a) * NE + e
                if n:
                    put(here, there, rs, dev(ee=j))
                else:
                    local(here, there, rs)

    backward(0)
    backward(1)
    scatter_x.forward()
    backward(2)
    scatter_x.finish()
    rj = lax.broadcasted_iota(jnp.int32, (128, 96), 0)
    cj = lax.broadcasted_iota(jnp.int32, (128, 96), 1)
    keep = jnp.logical_and((rj >> 4) * 12 + (rj & 15) == cj, (rj & 15) < 12)
    spread = jnp.where(keep, 1.0, 0.0).astype(BF)
    for i in range(2):
        for zz in range(NZH):
            block = r["gb"][i, x, pl.ds(zz * 96, 96), :]
            r["gy"][i, zz] = mm(spread, block).astype(BF).reshape(NY, 32, E)
    scatter_y.start_far()
    scatter_y.start_near()
    scatter_y.forward()
    scatter_y.finish()
    gz_sem = sems(8)
    for n in range(8):
        i = lax.rem(side + n // 4, 2)
        zz = lax.rem(zh + (n // 2) % 2, NZH)
        cc = lax.rem(c + n % 2, 2)
        put(
            r["gy"].at[i, zz, y, row(cc * 16, 16)],
            r["gz"].at[zh * NE + e],
            gz_sem + zh * NE + e,
            dev(ee=c * 2 + i, zz=zz, cc=cc),
            (half == c) if n == 0 else None,
        )
    for n in range(8):
        wait(r["gz"].at[n], gz_sem + n)
    total = r["gz"][0].astype(F32)
    for n in range(1, 8):
        total = total + r["gz"][n].astype(F32)
    wg[...] = total

    for p in range(3):
        for i in range(2):
            w = col(o * E + i * HW + p * PW, PW)
            wait(dres.at[0, :, col(c * E + i * HW + p * PW, PW)], dr_sem + p * 2 + i)
            wait(dres.at[0, :, w], dr_sem + 6 + p * 2 + i)
    for p in range(3):
        for a, (_, dst) in enumerate(grads):
            for j in range(NE):
                wait(
                    dst.at[0, :, pl.ds(j * HW + p * PW, PW)],
                    out_sem + (p * 3 + a) * NE + j,
                )
    for away, copy in pending:
        if away is None:
            copy.wait_send()
        else:
            pl.when(away)(copy.wait_send)


def per_device(q, k, v, res, ups, enc, gain, bias, weight, pm):
    wpad = jnp.pad(weight, ((0, 4), (0, 0)))
    hbm = pl.BlockSpec(memory_space=pl.ANY)
    vmem = pl.BlockSpec(memory_space=pltpu.VMEM)
    shape = jax.ShapeDtypeStruct((1, TOK, D), BF)
    outs = pl.pallas_call(
        kernel,
        out_shape=[shape] * 4 + [jax.ShapeDtypeStruct((16, E), F32)],
        in_specs=[hbm] * 6 + [vmem] * 4,
        out_specs=[hbm] * 4 + [vmem],
        scratch_shapes=[pltpu.VMEM(*spec) for spec in SCRATCH.values()]
        + [pltpu.SemaphoreType.DMA((NSEM,))],
        compiler_params=pltpu.CompilerParams(
            collective_id=0, has_side_effects=True, vmem_limit_bytes=56 * 2**20
        ),
        name="align_step",
    )(q, k, v, res, ups, enc, gain.reshape(1, E), bias.reshape(1, E), wpad, pm)
    return (*outs[:4], outs[4][:12])


def solution(mesh):
    token = P("seq", "enc", None)
    rows = P(("enc", "seq"), None)
    return jax.shard_map(
        per_device,
        mesh=mesh,
        in_specs=(token,) * 6 + (P(), P(), rows, P("seq", "enc")),
        out_specs=(token,) * 4 + (rows,),
        check_vma=False,
    )
```

time: 785 us -> 202 us (0.26); the launches traced: 774 us -> 200 us
  blocking collectives: 246 us -> 0 us
  Pallas kernels: 0 us -> 189 us
  starting transfers between devices: 142 us -> 0 us
  other arithmetic: 133 us -> 0 us
  local copies, waits for them, and re-layouts: 119 us -> 9.9 us
  waiting for transfers between devices: 90 us -> 0 us
  matrix products: 28.6 us -> 0 us
  between operations: 15.4 us -> 0.66 us
    unnamed x1 -> x0, blocking collectives: 214 us -> none
    pallas_call x0 -> x1, Pallas kernels: none -> 189 us  [per_device(): pl.pallas_call(kernel, out_shape=[shape] * 4 + [jax.ShapeDtypeStruct((16,...]
    unnamed x9 -> x0, other arithmetic: 112 us -> none
    unnamed x16 -> x0, starting transfers between devices: 87.8 us -> none
    unnamed x96 -> x15, local copies, waits for them, and re-layouts: 88 us -> 6.58 us
    reduce_scatter x1 -> x0, waiting for transfers between devices: 66.3 us -> none  [per_device(): lax.psum_scatter(jnp.einsum('tfd,de->tfe', flipped, weight_rows, preferre...]
    all_to_all x8 -> x0, starting transfers between devices: 53.7 us -> none  [the longest x1 9.74 us: per_device(): lax.all_to_all(residual_in, 'enc', split_axis=2, concat_axis=1, tiled=True)]
    all_to_all x1 -> x0, blocking collectives: 32.6 us -> none  [per_device(): lax.all_to_all(upstream, 'enc', split_axis=2, concat_axis=1, tiled=True)]
  transfers between devices with their start and end apart: 28 -> 0, of which waited for: 7 -> 0; matrix products, arithmetic and copies ran while one was open for 60% -> 0% of each run, Pallas kernels for 0% -> 0%
where the time goes in v1:
time: 202 us; the launch traced here: 200 us
  Pallas kernels  189 us (94%)
  local copies, waits for them, and re-layouts  9.9 us (5%)
    pallas_call x1, Pallas kernels, per_device(): pl.pallas_call(kernel, out_shape=[shape] * 4 + [jax.ShapeDtypeStruct((16,...  189 us
    unnamed x15, local copies, waits for them, and re-layouts  6.58 us

profile of v1, /device:TPU:34, one launch (start us, length us, event | category | flops | bytes accessed | tf_op | source)
XLA Modules:
  0.0 199.8 jit_solution(2508531052591939261)
XLA Ops:
  0.6 0.0 copy-start.4
  0.6 1.3 reshape.16.gain
  1.9 0.0 copy-done.4
  1.9 0.6 reshape.17.bias
  2.5 1.4 pad.4.wpad
  4.0 189.2 %align_step.1 = (bf16[1,128,3072]{2,1,0:T(8,128)(2,1)}, bf16[1,128,3072]{2,1,0:T(8,128)(2,1)}, bf16[1,128,3072]{2,1,0:T(8,128)(2,1)}, bf16[1,128,3072]{2,1,0:T(8,128)(2,1)}, f32[16,1536]{1,0:T(8,128)}) custom-call(bf16[1,128,3072]{2,1,0:T(8,128)(2,1)} %q.1, bf16[1,128,3072]{2,1,0:T(8,128)(2,1)} %k.1, bf16[1,128,3072]{2,1,0:T(8,128)(2,1)} %v.1, ...), custom_call_target="tpu_custom_call" | custom-call | tf_op jit(solution)/shard_map/align_step/pallas_call | solution.py:629
  193.2 0.0 copy-start.2
  193.2 2.1 %copy.20 = bf16[1,128,3072]{2,1,0:T(8,128)(2,1)} copy(bf16[1,128,3072]{2,1,0:T(8,128)(2,1)} %get-tuple-element.20) | data formatting | bytes 1572864
  195.4 0.0 copy-done.2
  195.4 0.0 copy-start.1
  195.4 0.9 copy.21
  196.2 0.5 copy-done.1
  196.8 0.0 copy-start
  196.8 0.9 copy.22
  197.7 0.5 copy-done
  198.2 0.0 copy-start.3
  198.2 0.9 copy.23
  199.1 0.1 copy-done.3
  199.2 0.6 copy.24
Async XLA Ops:
  0.6 1.3 copy-start.4
  193.2 2.1 %copy-start.2 = (bf16[1,128,3072]{2,1,0:T(8,128)(2,1)S(1)}, bf16[1,128,3072]{2,1,0:T(8,128)(2,1)}, u32[]{:S(2)}) copy-start(bf16[1,128,3072]{2,1,0:T(8,128)(2,1)} %get-tuple-element.21) | copy-start | bytes 2359300
  195.4 1.4 copy-start.1
  196.8 1.4 copy-start
  198.2 1.0 copy-start.3

commit v2 on v1

v2 whole, which is shorter than its diff:
```python
import math

import jax
import jax.numpy as jnp
from jax import lax
from jax.experimental import pallas as pl
from jax.experimental.pallas import tpu as pltpu
from jax.sharding import PartitionSpec as P

HD = 128
D = 3072
E = 1536
FT = 512
TOK = 128
HALF = 64
HW = 768
PW = 256
QUARTER = 384
NX, NY, NZH, NE = 4, 4, 2, 4
ALIGN = 128.0
EPS = 1e-6
SCALE = HD**-0.5
SCALE2 = SCALE * math.log2(math.e)
BF = jnp.bfloat16
F32 = jnp.float32
NT = (((1,), (1,)), ((), ()))
NN = (((1,), (0,)), ((), ()))


def mm(a, b, dims=NN):
    return lax.dot_general(a, b, dims, preferred_element_type=F32)


SCRATCH = {
    "encv": ((TOK, E), BF),
    "qh": ((FT, HW), BF),
    "kh": ((FT, HW), BF),
    "vh": ((FT, HW), BF),
    "pt": ((6, FT, FT), BF),
    "ob": ((FT, HW), BF),
    "oh": ((2 * TOK, E), BF),
    "rh": ((2 * TOK, E), BF),
    "uh": ((2 * TOK, E), BF),
    "hid": ((2 * TOK, E), BF),
    "hidt": ((E, 2 * TOK), BF),
    "hidp": ((NZH, 384, 2 * TOK), BF),
    "za": ((2 * TOK, E), F32),
    "zr": ((TOK, E), F32),
    "ts": ((TOK, E), BF),
    "tsl": ((FT, QUARTER), BF),
    "tpm": ((FT, QUARTER), BF),
    "tg": ((TOK, E), BF),
    "pmb": ((NE, 8, 128), jnp.int32),
    "pmo": ((8, 128), jnp.int32),
    "wp": ((2, NX, NZH, NY, 32, E), BF),
    "wh": ((E, E), BF),
    "wt": ((E, E), BF),
    "dzb": ((2 * TOK, E), BF),
    "drs": ((2 * TOK, E), BF),
    "doh": ((FT, HW), BF),
    "dqb": ((FT, HW), BF),
    "dkb": ((FT, HW), BF),
    "dvb": ((FT, HW), BF),
    "gka": ((FT, HW), F32),
    "gva": ((FT, HW), F32),
    "g0": ((NX, NZH, 96, E), BF),
    "t0": ((NZH, 96, E), BF),
    "l0": ((4, 96, E), BF),
    "gs": ((2, NX, NZH, NY, 32, E), BF),
    "g1": ((NZH, NY, 96, E), BF),
    "t1": ((NZH, 96, E), BF),
    "l1": ((4, 96, E), BF),
    "u0": ((NZH, 32, E), BF),
    "m0": ((4, 32, E), BF),
    "u1": ((NZH, 32, E), BF),
    "m1": ((4, 32, E), BF),
    "gz": ((4, 32, E), BF),
    "gt": ((32, E), BF),
    "gf": ((2, 16, E), BF),
    "wo": ((16, E), BF),
}
NSEM = 133


def kernel(
    q, k, v, res, ups, enc, gain, bias, weight, pm, dq, dk, dv, dres, wg, *scratch
):
    r = dict(zip(SCRATCH, scratch[: len(SCRATCH)], strict=True))
    sem = scratch[len(SCRATCH)]
    top = [0]

    def sems(n):
        base = top[0]
        top[0] += n
        assert top[0] <= NSEM
        return base

    e = lax.axis_index("enc")
    s = lax.axis_index("seq")
    c = lax.rem(s, 2)
    y = lax.rem(s // 2, NY)
    zh = lax.rem(s // 8, NZH)
    x = s // 16
    o = 1 - c
    half = e // 2
    side = lax.rem(e, 2)

    def seq_of(xx, zz, yy, cc):
        return ((xx * NZH + zz) * NY + yy) * 2 + cc

    def dev(ee=None, xx=None, zz=None, yy=None, cc=None):
        return (
            e if ee is None else ee,
            seq_of(
                x if xx is None else xx,
                zh if zz is None else zz,
                y if yy is None else yy,
                c if cc is None else cc,
            ),
        )

    sibling = dev(cc=o)
    line = tuple(lax.rem(e + n, NE) for n in range(NE))
    groups = {}

    class Group:
        def __init__(self, cond):
            self.sem, self.size, self.cond, self.done = sems(1), 0, cond, False

        def add(self, src):
            assert not self.done
            self.size += math.prod(src.shape) * src.dtype.itemsize

    def put(src, dst, rs, target, name, here=None):
        cond = None if here is None else jnp.logical_not(here)
        if name not in groups:
            groups[name] = Group(cond)
        group = groups[name]
        group.add(src)
        copy = pltpu.make_async_remote_copy(
            src_ref=src,
            dst_ref=dst,
            send_sem=sem.at[group.sem],
            recv_sem=sem.at[rs],
            device_id=target,
            device_id_type=pl.DeviceIdType.MESH,
        )
        if here is None:
            copy.start()
            return

        @pl.when(here)
        def _():
            pltpu.make_async_copy(src, dst, sem.at[rs]).start()

        @pl.when(cond)
        def _():
            copy.start()

    def flush(*names):
        for name in names:
            group = groups[name]
            group.done = True
            if group.size % (16 * E * 2):
                assert group.size % (8 * 128 * 4) == 0
                like = r["pmb"].at[pl.ds(0, group.size // (8 * 128 * 4))]
            else:
                like = r["wh"].at[pl.ds(0, group.size // (E * 2))]
            copy = pltpu.make_async_copy(like, like, sem.at[group.sem])
            if group.cond is None:
                copy.wait()
            else:
                pl.when(group.cond)(copy.wait)

    def local(src, dst, rs):
        pltpu.make_async_copy(src, dst, sem.at[rs]).start()

    def wait(dst, rs):
        pltpu.make_async_copy(dst, dst, sem.at[rs]).wait()

    def col(start, width):
        return pl.ds(pl.multiple_of(start, 128), width)

    def row(start, width):
        return pl.ds(pl.multiple_of(start, 16), width)

    barrier = pltpu.get_barrier_semaphore()
    mine = (zh * NE + e) * 2 + c
    greeted = []
    for n in range(1, 16):
        other = lax.rem(mine + n, 16)
        greeted.append(
            dev(ee=lax.rem(other // 2, NE), zz=other // 8, cc=lax.rem(other, 2))
        )
    for step in (1, 3):
        greeted.append(dev(yy=lax.rem(y + step, NY)))
        greeted.append(dev(xx=lax.rem(x + step, NX)))
    for target in greeted:
        pl.semaphore_signal(
            barrier, inc=1, device_id=target, device_id_type=pl.DeviceIdType.MESH
        )

    enc_sem = sems(1)
    local(enc.at[0], r["encv"], enc_sem)
    kv_sem, q_sem = sems(6), sems(6)
    pairs = ((k, r["kh"]), (v, r["vh"]))

    def move_kv(p, a, j, n):
        src, dst = pairs[a]
        src = src.at[0, :, col(j * HW + p * PW, PW)]
        dst = dst.at[row(e * TOK, TOK), pl.ds(p * PW, PW)]
        rs = kv_sem + p * 2 + a
        if n:
            put(src, dst, rs, dev(ee=j), "kv")
        else:
            local(src, dst, rs)

    def move_q(b, p, j, n):
        src = q.at[0, pl.ds(b * HALF, HALF), col(j * HW + p * PW, PW)]
        dst = r["qh"].at[row(b * 256 + e * HALF, HALF), pl.ds(p * PW, PW)]
        rs = q_sem + b * 3 + p
        if n:
            put(src, dst, rs, dev(ee=j), "q")
        else:
            local(src, dst, rs)

    for p in range(3):
        for a in range(2):
            move_kv(p, a, e, 0)
        for b in range(2):
            move_q(b, p, e, 0)
    half_sem = sems(4)
    mine_half = []
    for b in range(2):
        for a, (src, dst) in enumerate(((res, r["rh"]), (ups, r["uh"]))):
            from_rows, to_rows = pl.ds(b * HALF, HALF), row(b * TOK + c * HALF, HALF)
            local(
                src.at[0, from_rows, col(c * E, E)],
                dst.at[to_rows],
                half_sem + b * 2 + a,
            )
            mine_half.append(
                (
                    src.at[0, from_rows, col(o * E, E)],
                    dst.at[to_rows],
                    half_sem + b * 2 + a,
                )
            )

    rj = lax.broadcasted_iota(jnp.int32, (16, 12), 0)
    cj = lax.broadcasted_iota(jnp.int32, (16, 12), 1)
    pad = jnp.where(rj == cj, 1.0, 0.0).astype(BF)
    r["wo"][...] = mm(pad, weight[...]).astype(BF)

    pl.semaphore_wait(barrier, len(greeted))

    far_side = lax.rem(side + half + c, 2)
    w_sem = sems(1)
    shard = r["wp"].at[side, x, zh, y, row(c * 16, 16)]
    put(r["wo"], shard, w_sem, dev(ee=3 - e, cc=half), "w mirror")
    put(r["wo"], shard, w_sem, dev(cc=half), "w own", half == c)
    camp = [
        (lax.rem(zh + n // 2, NZH), lax.rem(half + n // 2, 2), lax.rem(side + n, 2))
        for n in range(4)
    ]

    def send_kv(p):
        for n in range(1, NE):
            for a in range(2):
                move_kv(p, a, line[n], n)

    def send_q(b, p):
        for n in range(1, NE):
            move_q(b, p, line[n], n)

    send_kv(0)
    send_q(0, 0)
    w2_sem = sems(4)
    held = r["wp"].at[far_side, x, zh, y]
    wait(held, w_sem)
    for n, (zz, hh, sd) in enumerate(camp):
        if n:
            put(held, held, w2_sem + zh * 2 + side, dev(ee=hh * 2 + sd, zz=zz), "w")
    for src, dst, rs in mine_half:
        put(src, dst, rs, sibling, "half")

    wait(r["encv"], enc_sem)
    r["pmo"][...] = jnp.broadcast_to(pm[...], (8, 128))

    gain_row, bias_row = gain[...].reshape(1, E), bias[...].reshape(1, E)

    def norm(i, _):
        rows = row(i * 32, 32)
        t = r["encv"][rows, :].astype(F32)
        mean = jnp.mean(t, axis=-1, keepdims=True)
        t = t - mean
        var = jnp.mean(t * t, axis=-1, keepdims=True)
        r["ts"][rows, :] = (t * lax.rsqrt(var + EPS) * gain_row + bias_row).astype(BF)
        return 0

    lax.fori_loop(0, TOK // 32, norm, 0)
    t_sem, pm_sem = sems(1), sems(1)
    for n in (1, 2, 3, 0):
        j = line[n]
        src = r["ts"].at[:, col(j * QUARTER, QUARTER)]
        dst = r["tsl"].at[row(e * TOK, TOK)]
        if n:
            put(src, dst, t_sem, dev(ee=j), "t")
            put(r["pmo"], r["pmb"].at[e], pm_sem, dev(ee=j), "pm")
        else:
            local(src, dst, t_sem)
            local(r["pmo"], r["pmb"].at[e], pm_sem)
    send_kv(1)
    send_q(0, 1)

    class Gather:
        def __init__(self, name, m, to, piece):
            self.name, self.m, self.to, self.piece = name, m, to, piece
            self.sem = sems(6)
            self.up, self.down = lax.rem(m + 1, 4), lax.rem(m + 3, 4)

        def start(self):
            for i in range(2):
                own = self.piece(self.m, i)
                put(own, own, self.sem + i, self.to(self.up), self.name)
                put(own, own, self.sem + 2 + i, self.to(self.down), self.name)

        def forward(self):
            first = self.piece(self.down, 0)
            wait(first, self.sem)
            put(first, first, self.sem + 4, self.to(self.up), self.name)
            second = self.piece(self.up, 1)
            wait(second, self.sem + 3)
            put(second, second, self.sem + 5, self.to(self.down), self.name)

        def finish(self):
            wait(self.piece(self.down, 1), self.sem + 1)
            wait(self.piece(self.up, 0), self.sem + 2)
            far = lax.rem(self.m + 2, 4)
            wait(self.piece(far, 0), self.sem + 4)
            wait(self.piece(far, 1), self.sem + 5)

    def to_x(m):
        return dev(xx=m)

    def to_y(m):
        return dev(yy=m)

    for n, (zz, hh, sd) in enumerate(camp):
        if n:
            i = lax.rem(sd + hh + c, 2)
            wait(r["wp"].at[i, x, zz, y], w2_sem + zz * 2 + sd)
    gather_y0 = Gather("gather y0", y, to_y, lambda m, i: r["wp"].at[0, x, i, m])
    gather_x1 = Gather("gather x1", x, to_x, lambda m, i: r["wp"].at[1, m, i, y])
    gather_x0 = Gather(
        "gather x0", x, to_x, lambda m, i: r["wh"].at[row(m * 192 + i * 96, 96)]
    )
    gather_y1 = Gather("gather y1", y, to_y, lambda m, i: r["wp"].at[1, :, i, m])
    ri = lax.broadcasted_iota(jnp.int32, (96, 128), 0)
    ci = lax.broadcasted_iota(jnp.int32, (96, 128), 1)
    keep = jnp.logical_and((ci >> 4) * 12 + (ci & 15) == ri, (ci & 15) < 12)
    squeeze = jnp.where(keep, 1.0, 0.0).astype(BF)

    def squeeze_block(i, xx, zz):
        block = r["wp"][i, xx, zz].reshape(128, E)
        r["wh"][row(i * HW + xx * 192 + zz * 96, 96), :] = mm(squeeze, block).astype(BF)

    gather_y0.start()
    gather_x1.start()
    gather_y0.forward()
    gather_x1.forward()
    gather_y0.finish()
    for zz in range(NZH):
        squeeze_block(0, x, zz)
    gather_x0.start()
    gather_x1.finish()
    gather_y1.start()

    o_sem = sems(2 * 3 * 2)

    def forward(b, p):
        if b == 0:
            for a, (_, dst) in enumerate(pairs):
                wait(dst.at[:, pl.ds(p * PW, PW)], kv_sem + p * 2 + a)
        wait(r["qh"].at[pl.ds(b * 256, 256), pl.ds(p * PW, PW)], q_sem + b * 3 + p)

        def head(hh, _):
            h = p * 2 + hh
            cols = col(h * HD, HD)
            rows = pl.ds(b * 256, 256)
            sc = mm(r["kh"][:, cols], r["qh"][rows, cols], NT)
            ex = jnp.exp2((sc - jnp.max(sc, axis=0, keepdims=True)) * SCALE2)
            pr = (ex * (1.0 / jnp.sum(ex, axis=0, keepdims=True))).astype(BF)
            r["pt"][h, :, rows] = pr
            out = mm(jnp.transpose(r["vh"][:, cols]), pr)
            r["ob"][rows, cols] = jnp.transpose(out).astype(BF)
            return 0

        lax.fori_loop(0, 2, head, 0)
        for n in (1, 2, 3, 0):
            j = line[n]
            put(
                r["ob"].at[row(b * 256 + j * HALF, HALF), pl.ds(p * PW, PW)],
                r["oh"].at[row(b * TOK + c * HALF, HALF), col(side * HW + p * PW, PW)],
                o_sem + (b * 3 + p) * 2 + side,
                dev(ee=j, cc=half),
                "o" if n else "o own",
                None if n else half == c,
            )

    def hidden(b, p):
        rows = pl.ds(b * TOK, TOK)
        part = 0.0
        for i in range(2):
            cols = pl.ds(i * HW + p * PW, PW)
            wait(r["oh"].at[rows, cols], o_sem + (b * 3 + p) * 2 + i)
            hid = (r["rh"][rows, cols].astype(F32) + r["oh"][rows, cols].astype(F32)).astype(
                BF
            )
            r["hid"][rows, cols] = hid
            part = part + mm(hid, r["wh"][cols, :])
        if p == 0:
            r["za"][rows, :] = part
        else:
            r["za"][rows, :] += part

    z_sem = sems(2)
    dz_sem = sems(2)

    def ours(b):
        return row(b * TOK + c * HALF, HALF)

    def theirs(b):
        return row(b * TOK + o * HALF, HALF)

    def z_sum(b):
        if b == 0:
            for bb in range(2):
                for a, dst in enumerate((r["rh"], r["uh"])):
                    wait(dst.at[pl.ds(bb * TOK, TOK)], half_sem + bb * 2 + a)
        for p in range(3):
            hidden(b, p)
        put(
            r["za"].at[theirs(b)],
            r["zr"].at[pl.ds(b * HALF, HALF)],
            z_sem + b,
            sibling,
            "z",
        )

    def align(b):
        if b == 0:
            wait(r["tg"], tb_sem)
        wait(r["zr"].at[pl.ds(b * HALF, HALF)], z_sem + b)

        def rows_of(i, _):
            rows = row(b * HALF + i * 32, 32)
            at = row(b * TOK + c * HALF + i * 32, 32)
            z = r["za"][at, :] + r["zr"][rows, :]
            t = r["tg"][rows, :].astype(F32)
            nz = jnp.sqrt(jnp.sum(z * z, axis=-1, keepdims=True) + EPS)
            ny = jnp.sqrt(jnp.sum(t * t, axis=-1, keepdims=True) + EPS)
            cosine = jnp.sum(z * t, axis=-1, keepdims=True) / (nz * ny)
            r["dzb"][at, :] = (
                -ALIGN * (t * (1.0 / (nz * ny)) - z * (cosine / (nz * nz)))
            ).astype(BF)
            return 0

        lax.fori_loop(0, HALF // 32, rows_of, 0)
        put(r["dzb"].at[ours(b)], r["dzb"].at[ours(b)], dz_sem + b, sibling, "dz")

    do_sem, dr_sem = sems(2 * 3), sems(2)

    def back(b):
        wait(r["dzb"].at[theirs(b)], dz_sem + b)
        rows = pl.ds(b * TOK, TOK)
        dz = r["dzb"][rows, :]
        for p in range(3):
            for i in range(2):
                cols = pl.ds(i * HW + p * PW, PW)
                part = mm(dz, r["wt"][:, cols])
                r["drs"][rows, cols] = (r["uh"][rows, cols].astype(F32) + part).astype(BF)
                for f in (c, o):
                    put(
                        r["drs"].at[row(b * TOK + f * HALF, HALF), cols],
                        r["doh"].at[row(b * 256 + e * HALF, HALF), pl.ds(p * PW, PW)],
                        do_sem + b * 3 + p,
                        dev(ee=c * 2 + i, cc=f),
                        ("do even", "do odd")[i] if f is c else "do",
                        (c * 2 + i == e) if f is c else None,
                    )
        out = dres.at[0, pl.ds(b * HALF, HALF), col(c * E, E)]
        local(r["drs"].at[ours(b)], out, dr_sem + b)
        put(r["drs"].at[theirs(b)], out, dr_sem + b, sibling, "dres")

    dq_sem, dkv_sem = sems(2), sems(2)
    grads = ((r["dkb"], dk), (r["dvb"], dv))

    def backward(b, p):
        wait(r["doh"].at[pl.ds(b * 256, 256), pl.ds(p * PW, PW)], do_sem + b * 3 + p)

        def head(hh, _):
            h = p * 2 + hh
            cols = col(h * HD, HD)
            rows = pl.ds(b * 256, 256)
            go = r["doh"][rows, cols]
            dp = mm(r["vh"][:, cols], go, NT)
            low = r["pt"][h, :, rows]
            pr = low.astype(F32)
            dot = jnp.sum(pr * dp, axis=0, keepdims=True)
            ds = (pr * (dp - dot) * SCALE).astype(BF)
            gv = mm(low, go)
            gk = mm(ds, r["qh"][rows, cols])
            gq = mm(jnp.transpose(r["kh"][:, cols]), ds)
            r["dqb"][rows, cols] = jnp.transpose(gq).astype(BF)
            if b == 0:
                r["gva"][:, cols] = gv
                r["gka"][:, cols] = gk
            else:
                r["dvb"][:, cols] = (r["gva"][:, cols] + gv).astype(BF)
                r["dkb"][:, cols] = (r["gka"][:, cols] + gk).astype(BF)
            return 0

        lax.fori_loop(0, 2, head, 0)
        for n in (1, 2, 3, 0):
            j = line[n]
            here = r["dqb"].at[row(b * 256 + j * HALF, HALF), pl.ds(p * PW, PW)]
            there = dq.at[0, pl.ds(b * HALF, HALF), col(e * HW + p * PW, PW)]
            if n:
                put(here, there, dq_sem + b, dev(ee=j), "dq")
            else:
                local(here, there, dq_sem + b)
            if b == 0:
                continue
            for a, (src, dst) in enumerate(grads):
                here = src.at[row(j * TOK, TOK), pl.ds(p * PW, PW)]
                there = dst.at[0, :, col(e * HW + p * PW, PW)]
                if n:
                    put(here, there, dkv_sem + a, dev(ee=j), "dkv")
                else:
                    local(here, there, dkv_sem + a)

    di = lax.broadcasted_iota(jnp.int32, (384, 384), 0)
    si = lax.broadcasted_iota(jnp.int32, (384, 384), 1)

    def at_least(value, unit):
        return sum((value >= n * unit).astype(jnp.int32) for n in range(1, 4))

    dy = at_least(di, 96)
    dx = at_least(di - dy * 96, 24)
    swap = jnp.where(di + (dx - dy) * 72 == si, 1.0, 0.0).astype(BF)

    def prepare(b):
        rows = pl.ds(b * TOK, TOK)

        def transpose(i, _):
            cols = col(i * 256, 256)
            r["hidt"][row(i * 256, 256), rows] = jnp.transpose(r["hid"][rows, cols])
            return 0

        lax.fori_loop(0, 6, transpose, 0)
        for zz in range(NZH):
            block = jnp.concatenate(
                [
                    r["hidt"][pl.ds(HW + xx * 192 + zz * 96, 96), rows]
                    for xx in range(NX)
                ],
                axis=0,
            )
            r["hidp"][zz, :, rows] = mm(swap, block).astype(BF)

    forward(0, 0)
    send_kv(2)
    send_q(0, 2)

    tb_sem = sems(1)
    wait(r["tsl"], t_sem)
    wait(r["pmb"], pm_sem)

    def permute(j, _):
        names = r["pmb"][j][0:1, :]
        at = lax.broadcasted_iota(jnp.int32, (FT, TOK), 0)
        pick = jnp.where(at == names, 1.0, 0.0)
        pick = jnp.transpose(pick).astype(BF)
        r["tpm"][row(j * TOK, TOK), :] = mm(pick, r["tsl"][...]).astype(BF)
        return 0

    lax.fori_loop(0, NE, permute, 0)
    for n in (1, 2, 3, 0):
        j = line[n]
        src = r["tpm"].at[row(j * TOK, TOK)]
        dst = r["tg"].at[:, col(e * QUARTER, QUARTER)]
        if n:
            put(src, dst, tb_sem, dev(ee=j), "tb")
        else:
            local(src, dst, tb_sem)

    gather_x0.forward()
    gather_y1.forward()
    forward(0, 1)
    for p in range(3):
        send_q(1, p)
    gather_x0.finish()
    gather_y1.finish()

    def squeeze_side(n, _):
        squeeze_block(1, n // NZH, lax.rem(n, NZH))
        return 0

    lax.fori_loop(0, NX * NZH, squeeze_side, 0)

    def turn(i, _):
        rows = col(i * 256, 256)
        r["wt"][:, rows] = jnp.transpose(r["wh"][rows, :])
        return 0

    lax.fori_loop(0, 6, turn, 0)
    forward(0, 2)
    forward(1, 0)
    z_sum(0)
    forward(1, 1)
    align(0)
    forward(1, 2)
    back(0)
    prepare(0)
    backward(0, 0)
    z_sum(1)
    prepare(1)
    backward(0, 1)
    align(1)
    backward(0, 2)
    back(1)
    early = [name for name in groups if name not in ("dq",)]

    rj = lax.broadcasted_iota(jnp.int32, (128, 96), 0)
    cj = lax.broadcasted_iota(jnp.int32, (128, 96), 1)
    keep = jnp.logical_and((rj >> 4) * 12 + (rj & 15) == cj, (rj & 15) < 12)
    spread = jnp.where(keep, 1.0, 0.0).astype(BF)

    class Scatter:
        def __init__(self, name, m, to, piece, transit, arrive):
            self.name, self.m, self.to, self.piece = name, m, to, piece
            self.transit, self.arrive = transit, arrive
            self.sem = sems(6)
            self.up, self.down = lax.rem(m + 1, 4), lax.rem(m + 3, 4)
            self.far = lax.rem(m + 2, 4)

        def start_far(self):
            put(self.piece(self.far, 0), self.transit(0), self.sem, self.to(self.up), self.name)
            put(self.piece(self.far, 1), self.transit(1), self.sem + 1, self.to(self.down), self.name)

        def start_near(self):
            put(self.piece(self.up, 1), self.arrive(1), self.sem + 3, self.to(self.up), self.name)
            put(self.piece(self.down, 0), self.arrive(2), self.sem + 4, self.to(self.down), self.name)

        def add(self, into, *others):
            def step(n, _):
                at = into.at[..., col(n * 512, 512)]
                total = at[...].astype(F32)
                for other in others:
                    total += other[..., col(n * 512, 512)].astype(F32)
                at[...] = total.astype(BF)
                return 0

            lax.fori_loop(0, 3, step, 0)

        def forward(self):
            wait(self.transit(0), self.sem)
            self.add(self.piece(self.up, 0), self.transit(0))
            put(self.piece(self.up, 0), self.arrive(0), self.sem + 2, self.to(self.up), self.name)
            wait(self.transit(1), self.sem + 1)
            self.add(self.piece(self.down, 1), self.transit(1))
            put(self.piece(self.down, 1), self.arrive(3), self.sem + 5, self.to(self.down), self.name)

        def finish(self):
            for n in range(4):
                wait(self.arrive(n), self.sem + 2 + n)
            self.add(self.piece(self.m, 0), self.arrive(0), self.arrive(2))
            self.add(self.piece(self.m, 1), self.arrive(1), self.arrive(3))

    def scatter(name, m, to, piece, transit, arrive):
        return Scatter(
            name, m, to, piece, lambda i: r[transit].at[i], lambda n: r[arrive].at[n]
        )

    scatter_x0 = scatter("scatter x0", x, to_x, lambda m, i: r["g0"].at[m, i], "t0", "l0")
    scatter_y1 = scatter("scatter y1", y, to_y, lambda m, i: r["g1"].at[i, m], "t1", "l1")
    scatter_y0 = scatter("scatter y0", y, to_y, lambda m, i: r["gs"].at[0, x, i, m], "u0", "m0")
    scatter_x1 = scatter("scatter x1", x, to_x, lambda m, i: r["gs"].at[1, m, i, y], "u1", "m1")

    def partial1(n, _):
        m, zz = n // NZH, lax.rem(n, NZH)
        part = mm(r["hidp"][zz, row(m * 96, 96), :], r["dzb"][...])
        r["g1"][zz, m] = part.astype(BF)
        return 0

    def partial0(m):
        a = r["hidt"][row(m * 192, 192), :]
        part = mm(a, r["dzb"][...]).astype(BF)
        r["g0"][m] = part.reshape(NZH, 96, E)

    partial0(scatter_x0.far)
    scatter_x0.start_far()
    lax.fori_loop(0, NX * NZH, partial1, 0)
    scatter_y1.start_far()
    scatter_y1.start_near()
    partial0(scatter_x0.up)
    partial0(scatter_x0.down)
    scatter_x0.start_near()
    partial0(x)

    backward(1, 0)
    scatter_x0.forward()
    backward(1, 1)
    scatter_y1.forward()
    backward(1, 2)
    flush(*early)
    for b in range(2):
        wait(dres.at[0, pl.ds(b * HALF, HALF)], dr_sem + b)
    scatter_x0.finish()
    for zz in range(NZH):
        part = mm(spread, r["g0"][x, zz]).astype(BF)
        r["gs"][0, x, zz] = part.reshape(NY, 32, E)
    scatter_y0.start_far()
    scatter_y0.start_near()
    scatter_y1.finish()
    for zz in range(NZH):
        part = mm(spread, r["g1"][zz, y]).astype(BF)
        r["gs"][1, :, zz, y] = part.reshape(NX, 32, E)
    scatter_x1.start_far()
    scatter_x1.start_near()
    scatter_y0.forward()
    scatter_x1.forward()
    scatter_y0.finish()
    scatter_x1.finish()
    gz_sem, gf_sem = sems(1), sems(1)
    for n, (zz, hh, sd) in enumerate(camp):
        i = lax.rem(sd + hh + c, 2)
        src, dst = r["gs"].at[i, x, zz, y], r["gz"].at[zh * 2 + side]
        if n:
            put(src, dst, gz_sem, dev(ee=hh * 2 + sd, zz=zz), "gz")
        else:
            local(src, dst, gz_sem)
    flush("scatter x0", "scatter y1", "scatter y0", "scatter x1")
    wait(r["gz"], gz_sem)
    total = r["gz"][0].astype(F32)
    for n in range(1, 4):
        total = total + r["gz"][n].astype(F32)
    r["gt"][...] = total.astype(BF)
    home = half == c
    where = jnp.where(home, e, 3 - e)
    slot = jnp.where(home, 0, 1)
    for cc in range(2):
        put(
            r["gt"].at[pl.ds(cc * 16, 16)],
            r["gf"].at[slot],
            gf_sem,
            dev(ee=where, cc=cc),
            ("gf 0", "gf 1")[cc],
            jnp.logical_and(home, c == cc),
        )
    wait(r["gf"], gf_sem)
    wg[...] = r["gf"][0].astype(F32) + r["gf"][1].astype(F32)

    for b in range(2):
        wait(dq.at[0, pl.ds(b * HALF, HALF)], dq_sem + b)
    wait(dk.at[0], dkv_sem)
    wait(dv.at[0], dkv_sem + 1)
    flush(*(name for name, group in groups.items() if not group.done))


def hand_over(*refs):
    ins, outs, held, sem = refs[:5], refs[5:10], refs[10], refs[11]
    loads, stores = [], []
    for n in range(4):
        for i in range(2):
            rows, at = pl.ds(i * HALF, HALF), n * 2 + i
            loads.append(
                pltpu.make_async_copy(ins[n].at[0, rows], held.at[at], sem.at[at])
            )
            stores.append(
                pltpu.make_async_copy(held.at[at], outs[n].at[0, rows], sem.at[8 + at])
            )
    for load in loads:
        load.start()
    outs[4][...] = ins[4][0:12, :]
    for load, store in zip(loads, stores, strict=True):
        load.wait()
        store.start()
    for store in stores:
        store.wait()


def per_device(q, k, v, res, ups, enc, gain, bias, weight, pm):
    hbm = pl.BlockSpec(memory_space=pl.ANY)
    vmem = pl.BlockSpec(memory_space=pltpu.VMEM)
    shape = jax.ShapeDtypeStruct((1, TOK, D), BF)
    outs = pl.pallas_call(
        kernel,
        out_shape=[shape] * 4 + [jax.ShapeDtypeStruct((16, E), F32)],
        in_specs=[hbm] * 6 + [vmem] * 4,
        out_specs=[hbm] * 4 + [vmem],
        scratch_shapes=[pltpu.VMEM(*spec) for spec in SCRATCH.values()]
        + [pltpu.SemaphoreType.DMA((NSEM,))],
        compiler_params=pltpu.CompilerParams(
            collective_id=0, has_side_effects=True, vmem_limit_bytes=56 * 2**20
        ),
        name="align_step",
    )(q, k, v, res, ups, enc, gain, bias, weight, pm)
    return pl.pallas_call(
        hand_over,
        out_shape=[shape] * 4 + [jax.ShapeDtypeStruct((12, E), F32)],
        in_specs=[hbm] * 4 + [vmem],
        out_specs=[hbm] * 4 + [vmem],
        scratch_shapes=[pltpu.VMEM((8, HALF, D), BF), pltpu.SemaphoreType.DMA((16,))],
        compiler_params=pltpu.CompilerParams(vmem_limit_bytes=56 * 2**20),
        name="hand_over",
    )(*outs)


def solution(mesh):
    token = P("seq", "enc", None)
    rows = P(("enc", "seq"), None)
    return jax.shard_map(
        per_device,
        mesh=mesh,
        in_specs=(token,) * 6 + (P(), P(), rows, P("seq", "enc")),
        out_specs=(token,) * 4 + (rows,),
        check_vma=False,
    )
```

time: 202 us -> 174 us (0.86)
  Pallas kernels: 189 us -> 173 us
  local copies, waits for them, and re-layouts: 9.9 us -> 0 us
    pallas_call x1, Pallas kernels: 189 us -> 168 us  [per_device(): pl.pallas_call(kernel, out_shape=[shape] * 4 + [jax.ShapeDtypeStruct((16,...]
    unnamed x15 -> x0, local copies, waits for them, and re-layouts: 6.58 us -> none
    pallas_call x0 -> x1, Pallas kernels: none -> 4.32 us  [per_device(): pl.pallas_call(hand_over, out_shape=[shape] * 4 + [jax.ShapeDtypeStruct((...]
where the time goes in v2:
time: 174 us; the launch traced here: 173 us
  Pallas kernels  173 us (99%)
    pallas_call x1, Pallas kernels, per_device(): pl.pallas_call(kernel, out_shape=[shape] * 4 + [jax.ShapeDtypeStruct((16,...  168 us
    pallas_call x1, Pallas kernels, per_device(): pl.pallas_call(hand_over, out_shape=[shape] * 4 + [jax.ShapeDtypeStruct((...  4.32 us

profile of v2, /device:TPU:34, one launch (start us, length us, event | category | flops | bytes accessed | tf_op | source)
XLA Modules:
  0.0 173.4 jit_solution(5789729547804686482)
XLA Ops:
  0.6 168.3 %align_step.1 = (bf16[1,128,3072]{2,1,0:T(8,128)(2,1)}, bf16[1,128,3072]{2,1,0:T(8,128)(2,1)}, bf16[1,128,3072]{2,1,0:T(8,128)(2,1)}, bf16[1,128,3072]{2,1,0:T(8,128)(2,1)}, f32[16,1536]{1,0:T(8,128)}) custom-call(bf16[1,128,3072]{2,1,0:T(8,128)(2,1)} %q.1, bf16[1,128,3072]{2,1,0:T(8,128)(2,1)} %k.1, bf16[1,128,3072]{2,1,0:T(8,128)(2,1)} %v.1, ...), custom_call_target="tpu_custom_call" | custom-call | tf_op jit(solution)/shard_map/align_step/pallas_call | solution.py:798
  168.9 4.3 %hand_over.1 = (bf16[1,128,3072]{2,1,0:T(8,128)(2,1)}, bf16[1,128,3072]{2,1,0:T(8,128)(2,1)}, bf16[1,128,3072]{2,1,0:T(8,128)(2,1)}, bf16[1,128,3072]{2,1,0:T(8,128)(2,1)}, f32[12,1536]{1,0:T(8,128)}) custom-call(bf16[1,128,3072]{2,1,0:T(8,128)(2,1)} %get-tuple-element.10.refs_0_, bf16[1,128,3072]{2,1,0:T(8,128)(2,1)} %get-tuple-element.11.refs_1_, ...), custom_call_target="tpu_custom_call" | custom-call | tf_op jit(solution)/shard_map/hand_over/pallas_call | solution.py:810

commit v3 on v2

v3 whole, which is shorter than its diff:
```python
import math

import jax
import jax.numpy as jnp
from jax import lax
from jax.experimental import pallas as pl
from jax.experimental.pallas import tpu as pltpu
from jax.sharding import PartitionSpec as P

HD = 128
D = 3072
E = 1536
FT = 512
TOK = 128
HALF = 64
HW = 768
PW = 256
QUARTER = 384
NX, NY, NZH, NE = 4, 4, 2, 4
ALIGN = 128.0
EPS = 1e-6
SCALE = HD**-0.5
SCALE2 = SCALE * math.log2(math.e)
BF = jnp.bfloat16
F32 = jnp.float32
NT = (((1,), (1,)), ((), ()))
NN = (((1,), (0,)), ((), ()))


def mm(a, b, dims=NN):
    return lax.dot_general(a, b, dims, preferred_element_type=F32)


SCRATCH = {
    "encv": ((TOK, E), BF),
    "qh": ((FT, HW), BF),
    "kh": ((FT, HW), BF),
    "vh": ((FT, HW), BF),
    "pt": ((6, FT, FT), BF),
    "ob": ((FT, HW), BF),
    "oh": ((2 * TOK, E), BF),
    "rh": ((2 * TOK, E), BF),
    "uh": ((3 * TOK, E), BF),
    "hid": ((3 * TOK, E), BF),
    "hidt": ((E, 3 * TOK), BF),
    "hidp": ((NZH, 384, 3 * TOK), BF),
    "za": ((2 * TOK, E), F32),
    "zr": ((TOK, E), F32),
    "ts": ((TOK, E), BF),
    "tsl": ((FT, QUARTER), BF),
    "tpm": ((FT, QUARTER), BF),
    "tg": ((TOK, E), BF),
    "pmb": ((NE, 8, 128), jnp.int32),
    "pmo": ((8, 128), jnp.int32),
    "wp": ((2, NX, NZH, NY, 32, E), BF),
    "wh": ((E, E), BF),
    "wt": ((E, E), BF),
    "dzb": ((3 * TOK, E), BF),
    "drs": ((3 * TOK, E), BF),
    "doh": ((FT, HW), BF),
    "dqb": ((FT, HW), BF),
    "dkb": ((FT, HW), BF),
    "dvb": ((FT, HW), BF),
    "rwp": ((TOK, E), F32),
    "rwx": ((HALF, E), F32),
    "rwo": ((HALF, E), BF),
    "rwi": ((TOK, E), BF),
    "g0": ((NX, NZH, 96, E), BF),
    "t0": ((NZH, 96, E), BF),
    "l0": ((4, 96, E), BF),
    "g1": ((NZH, NY, 96, E), BF),
    "t1": ((NZH, 96, E), BF),
    "l1": ((4, 96, E), BF),
    "u0": ((NZH, 32, E), BF),
    "m0": ((4, 32, E), BF),
    "u1": ((NZH, 32, E), BF),
    "m1": ((4, 32, E), BF),
    "gz": ((4, 32, E), BF),
    "gt": ((32, E), BF),
    "gf": ((2, 16, E), BF),
    "wo": ((16, E), BF),
}
NSEM = 144


def kernel(
    q, k, v, res, ups, enc, gain, bias, weight, pm, dq, dk, dv, dres, wg, *scratch
):
    r = dict(zip(SCRATCH, scratch[: len(SCRATCH)], strict=True))
    r["gs"] = r["wp"]
    sem = scratch[len(SCRATCH)]
    top = [0]

    def sems(n):
        base = top[0]
        top[0] += n
        assert top[0] <= NSEM
        return base

    e = lax.axis_index("enc")
    s = lax.axis_index("seq")
    c = lax.rem(s, 2)
    y = lax.rem(s // 2, NY)
    zh = lax.rem(s // 8, NZH)
    x = s // 16
    o = 1 - c
    half = e // 2
    side = lax.rem(e, 2)
    mirror = 3 - e
    mate = half * 2 + 1 - side
    near = half == c
    far = jnp.logical_not(near)
    group = side * 2 + c

    def seq_of(xx, zz, yy, cc):
        return ((xx * NZH + zz) * NY + yy) * 2 + cc

    def dev(ee=None, xx=None, zz=None, yy=None, cc=None):
        return (
            e if ee is None else ee,
            seq_of(
                x if xx is None else xx,
                zh if zz is None else zz,
                y if yy is None else yy,
                c if cc is None else cc,
            ),
        )

    sibling = dev(cc=o)
    groups = {}

    class Group:
        def __init__(self, cond):
            self.sem, self.size, self.cond, self.done = sems(1), 0, cond, False

        def add(self, src):
            assert not self.done
            self.size += math.prod(src.shape) * src.dtype.itemsize

    def put(src, dst, rs, target, name, here=None, only=None):
        cond = only if here is None else jnp.logical_not(here)
        if name not in groups:
            groups[name] = Group(cond)
        group = groups[name]
        group.add(src)
        copy = pltpu.make_async_remote_copy(
            src_ref=src,
            dst_ref=dst,
            send_sem=sem.at[group.sem],
            recv_sem=sem.at[rs],
            device_id=target,
            device_id_type=pl.DeviceIdType.MESH,
        )
        if cond is None:
            copy.start()
            return
        if here is not None:

            @pl.when(here)
            def _():
                pltpu.make_async_copy(src, dst, sem.at[rs]).start()

        @pl.when(cond)
        def _():
            copy.start()

    def flush(*names):
        for name in names:
            group = groups[name]
            group.done = True
            if group.size % (16 * E * 2):
                assert group.size % (8 * 128 * 4) == 0
                like = r["pmb"].at[pl.ds(0, group.size // (8 * 128 * 4))]
            else:
                like = r["wh"].at[pl.ds(0, group.size // (E * 2))]
            copy = pltpu.make_async_copy(like, like, sem.at[group.sem])
            if group.cond is None:
                copy.wait()
            else:
                pl.when(group.cond)(copy.wait)

    def local(src, dst, rs):
        pltpu.make_async_copy(src, dst, sem.at[rs]).start()

    def wait(dst, rs):
        pltpu.make_async_copy(dst, dst, sem.at[rs]).wait()

    def col(start, width):
        return pl.ds(pl.multiple_of(start, 128), width)

    def row(start, width):
        return pl.ds(pl.multiple_of(start, 16), width)

    barrier = pltpu.get_barrier_semaphore()
    mine = (zh * NE + e) * 2 + c
    greeted = []
    for n in range(1, 16):
        other = lax.rem(mine + n, 16)
        greeted.append(
            dev(ee=lax.rem(other // 2, NE), zz=other // 8, cc=lax.rem(other, 2))
        )
    for step in (1, 3):
        greeted.append(dev(yy=lax.rem(y + step, NY)))
        greeted.append(dev(xx=lax.rem(x + step, NX)))
    for target in greeted:
        pl.semaphore_signal(
            barrier, inc=1, device_id=target, device_id_type=pl.DeviceIdType.MESH
        )

    enc_sem = sems(1)
    local(enc.at[0], r["encv"], enc_sem)
    res_sem, ups_sem = sems(1), sems(2)
    res_rows = row(jnp.where(near, 0, TOK), TOK)
    ups_rows = row(jnp.where(near, 0, 2 * TOK), TOK)
    ups_slot = ups_sem + jnp.where(near, 0, 1)
    local(res.at[0, :, col(c * E, E)], r["rh"].at[res_rows], res_sem)
    local(ups.at[0, :, col(c * E, E)], r["uh"].at[ups_rows], ups_slot)

    rj = lax.broadcasted_iota(jnp.int32, (16, 12), 0)
    cj = lax.broadcasted_iota(jnp.int32, (16, 12), 1)
    pad = jnp.where(rj == cj, 1.0, 0.0).astype(BF)
    r["wo"][...] = mm(pad, weight[...]).astype(BF)

    pl.semaphore_wait(barrier, len(greeted))

    far_side = lax.rem(side + half + c, 2)
    w_sem = sems(1)
    shard = r["wp"].at[side, x, zh, y, row(c * 16, 16)]
    put(r["wo"], shard, w_sem, dev(ee=3 - e, cc=half), "w mirror")
    put(r["wo"], shard, w_sem, dev(cc=half), "w own", half == c)
    camp = [
        (lax.rem(zh + n // 2, NZH), lax.rem(half + n // 2, 2), lax.rem(side + n, 2))
        for n in range(4)
    ]

    qkv_sem = sems(9)
    qkv = ((k, r["kh"]), (v, r["vh"]), (q, r["qh"]))
    workers = [(i, i2, dev(ee=c * 2 + i, cc=i2)) for i in range(2) for i2 in range(2)]

    def is_here(i, i2):
        return jnp.logical_and(c * 2 + i == e, c == i2)

    def send_qkv(p, which=(0, 1, 2)):
        for i, i2, target in workers:
            for a in which:
                src, dst = qkv[a]
                put(
                    src.at[0, :, pl.ds((i * 2 + i2) * HW + p * PW, PW)],
                    dst.at[row(e * TOK, TOK), pl.ds(p * PW, PW)],
                    qkv_sem + p * 3 + a,
                    target,
                    f"qkv {i} {i2}",
                    is_here(i, i2),
                )

    send_qkv(0, (0,))
    w2_sem = sems(4)
    held = r["wp"].at[far_side, x, zh, y]
    wait(held, w_sem)
    for n, (zz, hh, sd) in enumerate(camp):
        if n:
            put(held, held, w2_sem + zh * 2 + side, dev(ee=hh * 2 + sd, zz=zz), "w")
    send_qkv(0, (1, 2))
    put(res.at[0, :, col(o * E, E)], r["rh"].at[res_rows], res_sem, sibling, "res")
    put(ups.at[0, :, col(o * E, E)], r["uh"].at[ups_rows], ups_slot, sibling, "ups")

    wait(r["encv"], enc_sem)
    r["pmo"][...] = jnp.broadcast_to(pm[...], (8, 128))
    gain_row, bias_row = gain[...].reshape(1, E), bias[...].reshape(1, E)

    def norm(i, _):
        rows = row(i * 32, 32)
        t = r["encv"][rows, :].astype(F32)
        mean = jnp.mean(t, axis=-1, keepdims=True)
        t = t - mean
        var = jnp.mean(t * t, axis=-1, keepdims=True)
        r["ts"][rows, :] = (t * lax.rsqrt(var + EPS) * gain_row + bias_row).astype(BF)
        return 0

    lax.fori_loop(0, TOK // 32, norm, 0)
    t_sem, pm_sem = sems(1), sems(1)
    for i, i2, target in workers:
        put(
            r["ts"].at[:, pl.ds((i * 2 + i2) * QUARTER, QUARTER)],
            r["tsl"].at[row(e * TOK, TOK)],
            t_sem,
            target,
            f"t {i} {i2}",
            is_here(i, i2),
        )
        put(
            r["pmo"],
            r["pmb"].at[e],
            pm_sem,
            target,
            f"pm {i} {i2}",
            is_here(i, i2),
        )
    send_qkv(1)

    class Gather:
        def __init__(self, name, m, to, piece):
            self.name, self.m, self.to, self.piece = name, m, to, piece
            self.sem = sems(6)
            self.up, self.down = lax.rem(m + 1, 4), lax.rem(m + 3, 4)

        def start(self):
            for i in range(2):
                own = self.piece(self.m, i)
                put(own, own, self.sem + i, self.to(self.up), self.name)
                put(own, own, self.sem + 2 + i, self.to(self.down), self.name)

        def forward(self):
            first = self.piece(self.down, 0)
            wait(first, self.sem)
            put(first, first, self.sem + 4, self.to(self.up), self.name)
            second = self.piece(self.up, 1)
            wait(second, self.sem + 3)
            put(second, second, self.sem + 5, self.to(self.down), self.name)

        def finish(self):
            wait(self.piece(self.down, 1), self.sem + 1)
            wait(self.piece(self.up, 0), self.sem + 2)
            far = lax.rem(self.m + 2, 4)
            wait(self.piece(far, 0), self.sem + 4)
            wait(self.piece(far, 1), self.sem + 5)

    def to_x(m):
        return dev(xx=m)

    def to_y(m):
        return dev(yy=m)

    for n, (zz, hh, sd) in enumerate(camp):
        if n:
            i = lax.rem(sd + hh + c, 2)
            wait(r["wp"].at[i, x, zz, y], w2_sem + zz * 2 + sd)
    gather_y0 = Gather("gather y0", y, to_y, lambda m, i: r["wp"].at[0, x, i, m])
    gather_x1 = Gather("gather x1", x, to_x, lambda m, i: r["wp"].at[1, m, i, y])
    gather_x0 = Gather(
        "gather x0", x, to_x, lambda m, i: r["wh"].at[row(m * 192 + i * 96, 96)]
    )
    gather_y1 = Gather("gather y1", y, to_y, lambda m, i: r["g1"].at[i, m])
    ri = lax.broadcasted_iota(jnp.int32, (96, 128), 0)
    ci = lax.broadcasted_iota(jnp.int32, (96, 128), 1)
    keep = jnp.logical_and((ci >> 4) * 12 + (ci & 15) == ri, (ci & 15) < 12)
    squeeze = jnp.where(keep, 1.0, 0.0).astype(BF)

    def squeeze_block(i, xx, zz):
        block = r["wp"][i, xx, zz].reshape(128, E)
        r["wh"][row(i * HW + xx * 192 + zz * 96, 96), :] = mm(squeeze, block).astype(BF)

    gather_y0.start()
    gather_x1.start()
    gather_y0.forward()
    gather_x1.forward()
    gather_y0.finish()
    for zz in range(NZH):
        squeeze_block(0, x, zz)
    gather_x0.start()
    gather_x1.finish()
    for zz in range(NZH):
        block = r["wp"][1, :, zz, y].reshape(128, E)
        r["g1"][zz, y] = mm(squeeze, block).astype(BF)
    gather_y1.start()

    o_sem = sems(6)

    def forward(p):
        for a, (_, dst) in enumerate(qkv):
            wait(dst.at[:, pl.ds(p * PW, PW)], qkv_sem + p * 3 + a)

        def head(hh, _):
            h = p * 2 + hh
            cols = col(h * HD, HD)
            kk = r["kh"][:, cols]
            vt = jnp.transpose(r["vh"][:, cols])
            for t in range(2):
                rows = pl.ds(t * 256, 256)
                sc = mm(kk, r["qh"][rows, cols], NT)
                ex = jnp.exp2((sc - jnp.max(sc, axis=0, keepdims=True)) * SCALE2)
                pr = (ex * (1.0 / jnp.sum(ex, axis=0, keepdims=True))).astype(BF)
                r["pt"][h, :, rows] = pr
                r["ob"][rows, cols] = jnp.transpose(mm(vt, pr)).astype(BF)
            return 0

        lax.fori_loop(0, 2, head, 0)
        for chip, name, here in ((mate, "o", None), (e, "o own", side == c)):
            for slot, block in enumerate((chip, 3 - chip)):
                put(
                    r["ob"].at[row(block * TOK, TOK), pl.ds(p * PW, PW)],
                    r["oh"].at[pl.ds(slot * TOK, TOK), col(c * HW + p * PW, PW)],
                    o_sem + p * 2 + c,
                    dev(ee=chip, cc=side),
                    name,
                    here,
                )

    rx_sem, rw_sem = sems(1), sems(1)

    def residual_part():
        wait(r["rh"], res_sem)
        r["rwp"][...] = mm(r["rh"][pl.ds(TOK, TOK), :], r["wh"][...])
        put(r["rwp"].at[row(o * HALF, HALF)], r["rwx"], rx_sem, sibling, "rwx")

    def residual_sum():
        wait(r["rwx"], rx_sem)
        r["rwo"][...] = (r["rwp"][row(c * HALF, HALF), :] + r["rwx"][...]).astype(BF)
        put(
            r["rwo"],
            r["rwi"].at[row(c * HALF, HALF)],
            rw_sem,
            dev(ee=mirror, cc=1),
            "rwo",
        )

    both = pl.ds(0, 2 * TOK)
    first, second, third = (pl.ds(n * TOK, TOK) for n in range(3))
    z_sem, dz_sem = sems(1), sems(1)

    def z_sum():
        for p in range(3):
            part = 0.0
            for i in range(2):
                cols = pl.ds(i * HW + p * PW, PW)
                wait(r["oh"].at[:, cols], o_sem + p * 2 + i)
                r["hid"][first, cols] = (
                    r["rh"][first, cols].astype(F32) + r["oh"][first, cols].astype(F32)
                ).astype(BF)
                r["hid"][second, cols] = r["oh"][second, cols]
                part = part + mm(r["hid"][both, cols], r["wh"][cols, :])
            if p == 0:
                r["za"][...] = part
            else:
                r["za"][...] += part
        theirs = row(o * TOK, TOK)
        put(r["za"].at[theirs], r["zr"], z_sem, sibling, "z")
        r["hid"][third, :] = r["rh"][second, :]

    def align():
        wait(r["tg"], tb_sem)

        @pl.when(c == 1)
        def _():
            wait(r["rwi"], rw_sem)
            r["za"][second, :] += r["rwi"][...].astype(F32)

        wait(r["zr"], z_sem)

        def rows_of(i, _):
            rows, at = row(i * 32, 32), row(c * TOK + i * 32, 32)
            z = r["za"][at, :] + r["zr"][rows, :]
            t = r["tg"][rows, :].astype(F32)
            nz = jnp.sqrt(jnp.sum(z * z, axis=-1, keepdims=True) + EPS)
            ny = jnp.sqrt(jnp.sum(t * t, axis=-1, keepdims=True) + EPS)
            cosine = jnp.sum(z * t, axis=-1, keepdims=True) / (nz * ny)
            r["dzb"][at, :] = (
                -ALIGN * (t * (1.0 / (nz * ny)) - z * (cosine / (nz * nz)))
            ).astype(BF)
            return 0

        lax.fori_loop(0, TOK // 32, rows_of, 0)
        ours, theirs = row(c * TOK, TOK), row(o * TOK, TOK)
        put(r["dzb"].at[ours], r["dzb"].at[ours], dz_sem, sibling, "dz")
        wait(r["dzb"].at[theirs], dz_sem)

    home_sem, pass_sem = sems(1), sems(1)

    def send_home():
        put(
            r["dzb"].at[row(TOK + c * HALF, HALF)],
            r["dzb"].at[row(2 * TOK + c * HALF, HALF)],
            home_sem,
            dev(ee=mirror),
            "home",
        )

    def pass_on():
        rows = r["dzb"].at[row(2 * TOK + c * HALF, HALF)]
        wait(rows, home_sem)
        put(rows, rows, pass_sem, sibling, "pass")

    far_sem, do_sem, dr_sem = sems(6), sems(3), sems(1)

    def send_upstream():
        for p in range(3):
            for h in range(2):
                for i in range(2):
                    cols = pl.ds(i * HW + p * PW, PW)
                    put(
                        ups.at[0, :, pl.ds(h * E + i * HW + p * PW, PW)],
                        r["uh"].at[second, cols],
                        far_sem + p * 2 + i,
                        dev(ee=mirror, cc=h),
                        "far ups",
                        only=far,
                    )

    def back(p):
        if p == 0:
            wait(r["uh"].at[first], ups_sem)
        for i in range(2):
            cols = pl.ds(i * HW + p * PW, PW)
            part = mm(r["dzb"][both, :], r["wt"][:, cols])
            wait(r["uh"].at[second, cols], far_sem + p * 2 + i)
            r["drs"][both, cols] = (r["uh"][both, cols].astype(F32) + part).astype(BF)
            for slot, block in enumerate((e, mirror)):
                put(
                    r["drs"].at[pl.ds(slot * TOK, TOK), cols],
                    r["doh"].at[row(block * TOK, TOK), pl.ds(p * PW, PW)],
                    do_sem + p,
                    dev(ee=half * 2 + c, cc=i),
                    f"do {i}",
                    jnp.logical_and(side == c, c == i),
                )
        if p == 2:
            out = dres.at[0, :, col(c * E, E)]
            put(r["drs"].at[first], out, dr_sem, dev(cc=half), "dres 0", near)

    def back_far():
        wait(r["dzb"].at[row(2 * TOK + o * HALF, HALF)], pass_sem)
        wait(r["uh"].at[third], ups_sem + 1)

        def tile(n, _):
            cols = col(n * 512, 512)
            part = mm(r["dzb"][third, :], r["wt"][:, cols])
            r["drs"][third, cols] = (r["uh"][third, cols].astype(F32) + part).astype(BF)
            return 0

        lax.fori_loop(0, 3, tile, 0)
        out = dres.at[0, :, col(c * E, E)]
        put(r["drs"].at[third], out, dr_sem, dev(cc=1 - half), "dres 2", far)

    out_sem = sems(3)
    grads = ((r["dkb"], dk), (r["dvb"], dv), (r["dqb"], dq))

    def backward(p):
        wait(r["doh"].at[:, pl.ds(p * PW, PW)], do_sem + p)

        def head(hh, _):
            h = p * 2 + hh
            cols = col(h * HD, HD)
            vv = r["vh"][:, cols]
            kt = jnp.transpose(r["kh"][:, cols])
            gv = gk = 0.0
            for t in range(2):
                rows = pl.ds(t * 256, 256)
                go = r["doh"][rows, cols]
                dp = mm(vv, go, NT)
                low = r["pt"][h, :, rows]
                pr = low.astype(F32)
                dot = jnp.sum(pr * dp, axis=0, keepdims=True)
                ds = (pr * (dp - dot) * SCALE).astype(BF)
                gv = gv + mm(low, go)
                gk = gk + mm(ds, r["qh"][rows, cols])
                r["dqb"][rows, cols] = jnp.transpose(mm(kt, ds)).astype(BF)
            r["dvb"][:, cols] = gv.astype(BF)
            r["dkb"][:, cols] = gk.astype(BF)
            return 0

        lax.fori_loop(0, 2, head, 0)
        for n in range(NE):
            j = lax.rem(mirror + n, NE)
            for a, (src, dst) in enumerate(grads):
                put(
                    src.at[row(j * TOK, TOK), pl.ds(p * PW, PW)],
                    dst.at[0, :, col(group * HW + p * PW, PW)],
                    out_sem + a,
                    dev(ee=j, cc=half),
                    f"grad {n}",
                    jnp.logical_and(near, j == e),
                )

    di = lax.broadcasted_iota(jnp.int32, (384, 384), 0)
    si = lax.broadcasted_iota(jnp.int32, (384, 384), 1)

    def at_least(value, unit):
        return sum((value >= n * unit).astype(jnp.int32) for n in range(1, 4))

    dy = at_least(di, 96)
    dx = at_least(di - dy * 96, 24)
    swap = jnp.where(di + (dx - dy) * 72 == si, 1.0, 0.0).astype(BF)

    def prepare():
        def transpose(i, _):
            cols = col(i * 256, 256)
            r["hidt"][row(i * 256, 256), :] = jnp.transpose(r["hid"][:, cols])
            return 0

        lax.fori_loop(0, 6, transpose, 0)
        for zz in range(NZH):
            block = jnp.concatenate(
                [
                    r["hidt"][pl.ds(HW + xx * 192 + zz * 96, 96), :]
                    for xx in range(NX)
                ],
                axis=0,
            )
            r["hidp"][zz] = mm(swap, block).astype(BF)

    forward(0)
    send_qkv(2)

    tb_sem = sems(1)
    wait(r["tsl"], t_sem)
    wait(r["pmb"], pm_sem)

    def permute(j, _):
        names = r["pmb"][j][0:1, :]
        at = lax.broadcasted_iota(jnp.int32, (FT, TOK), 0)
        pick = jnp.where(at == names, 1.0, 0.0)
        pick = jnp.transpose(pick).astype(BF)
        r["tpm"][row(j * TOK, TOK), :] = mm(pick, r["tsl"][...]).astype(BF)
        return 0

    lax.fori_loop(0, NE, permute, 0)
    for chip in (mate, e):
        for slot, block in enumerate((chip, 3 - chip)):
            put(
                r["tpm"].at[row(block * TOK, TOK)],
                r["tg"].at[:, col(group * QUARTER, QUARTER)],
                tb_sem,
                dev(ee=chip, cc=slot),
                f"tb {slot}" if chip is e else "tb",
                c == slot if chip is e else None,
            )

    gather_x0.forward()
    gather_y1.forward()
    forward(1)
    gather_x0.finish()
    gather_y1.finish()

    def unswap(n, _):
        cols = col(n * 512, 512)
        for zz in range(NZH):
            block = r["g1"][zz, :, :, cols].reshape(384, 512)
            block = mm(swap, block).astype(BF)
            for xx in range(NX):
                rows = pl.ds(HW + xx * 192 + zz * 96, 96)
                r["wh"][rows, cols] = block[xx * 96 : xx * 96 + 96]
        return 0

    lax.fori_loop(0, 3, unswap, 0)
    residual_part()
    def turn(i, _):
        rows = col(i * 256, 256)
        r["wt"][:, rows] = jnp.transpose(r["wh"][rows, :])
        return 0

    lax.fori_loop(0, 6, turn, 0)
    residual_sum()

    forward(2)
    send_upstream()
    z_sum()
    prepare()
    align()
    send_home()
    back(0)
    back(1)
    backward(0)
    pass_on()
    back(2)
    backward(1)
    back_far()
    flush("gather y1")
    early = [
        name
        for name, sent in groups.items()
        if not sent.done and not name.startswith("grad")
    ]

    rj = lax.broadcasted_iota(jnp.int32, (128, 96), 0)
    cj = lax.broadcasted_iota(jnp.int32, (128, 96), 1)
    keep = jnp.logical_and((rj >> 4) * 12 + (rj & 15) == cj, (rj & 15) < 12)
    spread = jnp.where(keep, 1.0, 0.0).astype(BF)

    class Scatter:
        def __init__(self, name, m, to, piece, transit, arrive):
            self.name, self.m, self.to, self.piece = name, m, to, piece
            self.transit, self.arrive = transit, arrive
            self.sem = sems(6)
            self.up, self.down = lax.rem(m + 1, 4), lax.rem(m + 3, 4)
            self.far = lax.rem(m + 2, 4)

        def start_far(self):
            put(self.piece(self.far, 0), self.transit(0), self.sem, self.to(self.up), self.name)
            put(self.piece(self.far, 1), self.transit(1), self.sem + 1, self.to(self.down), self.name)

        def start_near(self):
            put(self.piece(self.up, 1), self.arrive(1), self.sem + 3, self.to(self.up), self.name)
            put(self.piece(self.down, 0), self.arrive(2), self.sem + 4, self.to(self.down), self.name)

        def add(self, into, *others):
            def step(n, _):
                at = into.at[..., col(n * 512, 512)]
                total = at[...].astype(F32)
                for other in others:
                    total += other[..., col(n * 512, 512)].astype(F32)
                at[...] = total.astype(BF)
                return 0

            lax.fori_loop(0, 3, step, 0)

        def forward(self):
            wait(self.transit(0), self.sem)
            self.add(self.piece(self.up, 0), self.transit(0))
            put(self.piece(self.up, 0), self.arrive(0), self.sem + 2, self.to(self.up), self.name)
            wait(self.transit(1), self.sem + 1)
            self.add(self.piece(self.down, 1), self.transit(1))
            put(self.piece(self.down, 1), self.arrive(3), self.sem + 5, self.to(self.down), self.name)

        def finish(self):
            for n in range(4):
                wait(self.arrive(n), self.sem + 2 + n)
            self.add(self.piece(self.m, 0), self.arrive(0), self.arrive(2))
            self.add(self.piece(self.m, 1), self.arrive(1), self.arrive(3))

    def scatter(name, m, to, piece, transit, arrive):
        return Scatter(
            name, m, to, piece, lambda i: r[transit].at[i], lambda n: r[arrive].at[n]
        )

    scatter_x0 = scatter("scatter x0", x, to_x, lambda m, i: r["g0"].at[m, i], "t0", "l0")
    scatter_y1 = scatter("scatter y1", y, to_y, lambda m, i: r["g1"].at[i, m], "t1", "l1")
    scatter_y0 = scatter("scatter y0", y, to_y, lambda m, i: r["gs"].at[0, x, i, m], "u0", "m0")
    scatter_x1 = scatter("scatter x1", x, to_x, lambda m, i: r["gs"].at[1, m, i, y], "u1", "m1")

    def partial1(n, _):
        m, zz = n // NZH, lax.rem(n, NZH)
        part = mm(r["hidp"][zz, row(m * 96, 96), :], r["dzb"][...])
        r["g1"][zz, m] = part.astype(BF)
        return 0

    def partial0(m):
        a = r["hidt"][row(m * 192, 192), :]
        part = mm(a, r["dzb"][...]).astype(BF)
        r["g0"][m] = part.reshape(NZH, 96, E)

    partial0(scatter_x0.far)
    scatter_x0.start_far()
    lax.fori_loop(0, NX * NZH, partial1, 0)
    scatter_y1.start_far()
    scatter_y1.start_near()
    partial0(scatter_x0.up)
    partial0(scatter_x0.down)
    scatter_x0.start_near()
    partial0(x)
    backward(2)
    flush(*early)
    scatter_x0.forward()
    scatter_y1.forward()
    wait(dres.at[0], dr_sem)
    scatter_x0.finish()
    for zz in range(NZH):
        part = mm(spread, r["g0"][x, zz]).astype(BF)
        r["gs"][0, x, zz] = part.reshape(NY, 32, E)
    scatter_y0.start_far()
    scatter_y0.start_near()
    scatter_y1.finish()
    for zz in range(NZH):
        part = mm(spread, r["g1"][zz, y]).astype(BF)
        r["gs"][1, :, zz, y] = part.reshape(NX, 32, E)
    scatter_x1.start_far()
    scatter_x1.start_near()
    scatter_y0.forward()
    scatter_x1.forward()
    scatter_y0.finish()
    scatter_x1.finish()
    gz_sem, gf_sem = sems(1), sems(1)
    for n, (zz, hh, sd) in enumerate(camp):
        i = lax.rem(sd + hh + c, 2)
        src, dst = r["gs"].at[i, x, zz, y], r["gz"].at[zh * 2 + side]
        if n:
            put(src, dst, gz_sem, dev(ee=hh * 2 + sd, zz=zz), "gz")
        else:
            local(src, dst, gz_sem)
    flush("scatter x0", "scatter y1", "scatter y0", "scatter x1")
    wait(r["gz"], gz_sem)
    total = r["gz"][0].astype(F32)
    for n in range(1, 4):
        total = total + r["gz"][n].astype(F32)
    r["gt"][...] = total.astype(BF)
    home = half == c
    where = jnp.where(home, e, 3 - e)
    slot = jnp.where(home, 0, 1)
    for cc in range(2):
        put(
            r["gt"].at[pl.ds(cc * 16, 16)],
            r["gf"].at[slot],
            gf_sem,
            dev(ee=where, cc=cc),
            ("gf 0", "gf 1")[cc],
            jnp.logical_and(home, c == cc),
        )
    wait(r["gf"], gf_sem)
    wg[...] = r["gf"][0].astype(F32) + r["gf"][1].astype(F32)

    for a, (_, dst) in enumerate(grads):
        wait(dst.at[0], out_sem + a)
    flush(*(name for name, sent in groups.items() if not sent.done))


def hand_over(*refs):
    ins, outs, sem = refs[:5], refs[5:10], refs[10]
    copies = [
        pltpu.make_async_copy(ins[n].at[0], outs[n].at[0], sem.at[n]) for n in range(4)
    ]
    for copy in copies:
        copy.start()
    outs[4][...] = ins[4][0:12, :]
    for copy in copies:
        copy.wait()


def per_device(q, k, v, res, ups, enc, gain, bias, weight, pm):
    hbm = pl.BlockSpec(memory_space=pltpu.HBM)
    anywhere = pl.BlockSpec(memory_space=pl.ANY)
    vmem = pl.BlockSpec(memory_space=pltpu.VMEM)
    shape = jax.ShapeDtypeStruct((1, TOK, D), BF)
    args = [
        pltpu.with_memory_space_constraint(a, pltpu.HBM)
        for a in (q, k, v, res, ups, enc, gain, bias, weight, pm)
    ]
    outs = pl.pallas_call(
        kernel,
        out_shape=[shape] * 4 + [jax.ShapeDtypeStruct((16, E), F32)],
        in_specs=[hbm] * 6 + [vmem] * 4,
        out_specs=[anywhere] * 4 + [vmem],
        scratch_shapes=[pltpu.VMEM(*spec) for spec in SCRATCH.values()]
        + [pltpu.SemaphoreType.DMA((NSEM,))],
        compiler_params=pltpu.CompilerParams(
            collective_id=0, has_side_effects=True, vmem_limit_bytes=50 * 2**20
        ),
        name="align_step",
    )(*args)
    return pl.pallas_call(
        hand_over,
        out_shape=[shape] * 4 + [jax.ShapeDtypeStruct((12, E), F32)],
        in_specs=[anywhere] * 4 + [vmem],
        out_specs=[hbm] * 4 + [vmem],
        scratch_shapes=[pltpu.SemaphoreType.DMA((4,))],
        compiler_params=pltpu.CompilerParams(vmem_limit_bytes=2**20),
        name="hand_over",
    )(*outs)


def solution(mesh):
    token = P("seq", "enc", None)
    rows = P(("enc", "seq"), None)
    return jax.shard_map(
        per_device,
        mesh=mesh,
        in_specs=(token,) * 6 + (P(), P(), rows, P("seq", "enc")),
        out_specs=(token,) * 4 + (rows,),
        check_vma=False,
    )
```

time: 174 us -> 170 us (0.977); the launches traced: 173 us -> 168 us
  Pallas kernels: 173 us -> 167 us
    pallas_call x1, Pallas kernels: 168 us -> 164 us  [per_device(): pl.pallas_call(kernel, out_shape=[shape] * 4 + [jax.ShapeDtypeStruct((16,...]
    pallas_call x1, Pallas kernels: 4.32 us -> 2.33 us  [per_device(): pl.pallas_call(hand_over, out_shape=[shape] * 4 + [jax.ShapeDtypeStruct((...]
where the time goes in v3:
time: 170 us; the launch traced here: 168 us
  Pallas kernels  167 us (98%)
    pallas_call x1, Pallas kernels, per_device(): pl.pallas_call(kernel, out_shape=[shape] * 4 + [jax.ShapeDtypeStruct((16,...  164 us

profile of v3, /device:TPU:34, one launch (start us, length us, event | category | flops | bytes accessed | tf_op | source)
XLA Modules:
  0.0 167.5 jit_solution(1747377271031905506)
XLA Ops:
  0.6 164.4 %align_step.1 = (bf16[1,128,3072]{2,1,0:T(8,128)(2,1)S(1)}, bf16[1,128,3072]{2,1,0:T(8,128)(2,1)S(1)}, bf16[1,128,3072]{2,1,0:T(8,128)(2,1)S(1)}, bf16[1,128,3072]{2,1,0:T(8,128)(2,1)S(1)}, f32[16,1536]{1,0:T(8,128)S(1)}) custom-call(bf16[1,128,3072]{2,1,0:T(8,128)(2,1)} %q.1, bf16[1,128,3072]{2,1,0:T(8,128)(2,1)} %k.1, bf16[1,128,3072]{2,1,0:T(8,128)(2,1)} %v.1, ...), custom_call_target="tpu_custom_call" | custom-call | tf_op jit(solution)/shard_map/align_step/pallas_call | solution.py:826
  165.0 2.3 %hand_over.1 = (bf16[1,128,3072]{2,1,0:T(8,128)(2,1)}, bf16[1,128,3072]{2,1,0:T(8,128)(2,1)}, bf16[1,128,3072]{2,1,0:T(8,128)(2,1)}, bf16[1,128,3072]{2,1,0:T(8,128)(2,1)}, f32[12,1536]{1,0:T(8,128)}) custom-call(bf16[1,128,3072]{2,1,0:T(8,128)(2,1)S(1)} %get-tuple-element.10.refs_0_, bf16[1,128,3072]{2,1,0:T(8,128)(2,1)S(1)} %get-tuple-element.11.refs_1_, ...), custom_call_target="tpu_custom_call" | custom-call | tf_op jit(solution)/shard_map/hand_over/pallas_call | solution.py:838

commit v4 on v3

--- a/solution.py
+++ b/solution.py
@@ -33,6 +33,9 @@
 
 SCRATCH = {
     "encv": ((TOK, E), BF),
+    "gainv": ((E,), F32),
+    "biasv": ((E,), F32),
+    "pmv": ((1, TOK), jnp.int32),
     "qh": ((FT, HW), BF),
     "kh": ((FT, HW), BF),
     "vh": ((FT, HW), BF),
@@ -80,7 +83,7 @@
     "gf": ((2, 16, E), BF),
     "wo": ((16, E), BF),
 }
-NSEM = 144
+NSEM = 147
 
 
 def kernel(
@@ -209,6 +212,10 @@
 
     enc_sem = sems(1)
     local(enc.at[0], r["encv"], enc_sem)
+    small_sem = sems(3)
+    small = ((gain, r["gainv"]), (bias, r["biasv"]), (pm, r["pmv"]))
+    for n, (src, dst) in enumerate(small):
+        local(src, dst, small_sem + n)
     res_sem, ups_sem = sems(1), sems(2)
     res_rows = row(jnp.where(near, 0, TOK), TOK)
     ups_rows = row(jnp.where(near, 0, 2 * TOK), TOK)
@@ -265,8 +272,10 @@
     put(ups.at[0, :, col(o * E, E)], r["uh"].at[ups_rows], ups_slot, sibling, "ups")
 
     wait(r["encv"], enc_sem)
-    r["pmo"][...] = jnp.broadcast_to(pm[...], (8, 128))
-    gain_row, bias_row = gain[...].reshape(1, E), bias[...].reshape(1, E)
+    for n, (_, dst) in enumerate(small):
+        wait(dst, small_sem + n)
+    r["pmo"][...] = jnp.broadcast_to(r["pmv"][...], (8, 128))
+    gain_row, bias_row = r["gainv"][...].reshape(1, E), r["biasv"][...].reshape(1, E)
 
     def norm(i, _):
         rows = row(i * 32, 32)
@@ -296,6 +305,7 @@
             f"pm {i} {i2}",
             is_here(i, i2),
         )
+
     send_qkv(1)
 
     class Gather:
@@ -599,7 +609,6 @@
             r["hidp"][zz] = mm(swap, block).astype(BF)
 
     forward(0)
-    send_qkv(2)
 
     tb_sem = sems(1)
     wait(r["tsl"], t_sem)
@@ -625,6 +634,7 @@
                 c == slot if chip is e else None,
             )
 
+    send_qkv(2)
     gather_x0.forward()
     gather_y1.forward()
     forward(1)
@@ -654,12 +664,12 @@
     forward(2)
     send_upstream()
     z_sum()
-    prepare()
     align()
     send_home()
     back(0)
     back(1)
     backward(0)
+    prepare()
     pass_on()
     back(2)
     backward(1)
@@ -826,7 +836,7 @@
     outs = pl.pallas_call(
         kernel,
         out_shape=[shape] * 4 + [jax.ShapeDtypeStruct((16, E), F32)],
-        in_specs=[hbm] * 6 + [vmem] * 4,
+        in_specs=[hbm] * 8 + [vmem, hbm],
         out_specs=[anywhere] * 4 + [vmem],
         scratch_shapes=[pltpu.VMEM(*spec) for spec in SCRATCH.values()]
         + [pltpu.SemaphoreType.DMA((NSEM,))],

time: 170 us -> 185 us (1.088)
  Pallas kernels: 167 us -> 181 us
    pallas_call x1, Pallas kernels: 164 us -> 179 us  [per_device(): pl.pallas_call(kernel, out_shape=[shape] * 4 + [jax.ShapeDtypeStruct((16,...]
where the time goes in v4:
time: 185 us; the launch traced here: 182 us
  Pallas kernels  181 us (98%)
    pallas_call x1, Pallas kernels, per_device(): pl.pallas_call(kernel, out_shape=[shape] * 4 + [jax.ShapeDtypeStruct((16,...  179 us

profile of v4, /device:TPU:34, one launch (start us, length us, event | category | flops | bytes accessed | tf_op | source)
XLA Modules:
  0.0 181.8 jit_solution(1956902846122893415)
XLA Ops:
  0.6 178.7 %align_step.1 = (bf16[1,128,3072]{2,1,0:T(8,128)(2,1)S(1)}, bf16[1,128,3072]{2,1,0:T(8,128)(2,1)S(1)}, bf16[1,128,3072]{2,1,0:T(8,128)(2,1)S(1)}, bf16[1,128,3072]{2,1,0:T(8,128)(2,1)S(1)}, f32[16,1536]{1,0:T(8,128)S(1)}) custom-call(bf16[1,128,3072]{2,1,0:T(8,128)(2,1)} %q.1, bf16[1,128,3072]{2,1,0:T(8,128)(2,1)} %k.1, bf16[1,128,3072]{2,1,0:T(8,128)(2,1)} %v.1, ...), custom_call_target="tpu_custom_call" | custom-call | tf_op jit(solution)/shard_map/align_step/pallas_call | solution.py:836
  179.3 2.3 %hand_over.1 = (bf16[1,128,3072]{2,1,0:T(8,128)(2,1)}, bf16[1,128,3072]{2,1,0:T(8,128)(2,1)}, bf16[1,128,3072]{2,1,0:T(8,128)(2,1)}, bf16[1,128,3072]{2,1,0:T(8,128)(2,1)}, f32[12,1536]{1,0:T(8,128)}) custom-call(bf16[1,128,3072]{2,1,0:T(8,128)(2,1)S(1)} %get-tuple-element.10.refs_0_, bf16[1,128,3072]{2,1,0:T(8,128)(2,1)S(1)} %get-tuple-element.11.refs_1_, ...), custom_call_target="tpu_custom_call" | custom-call | tf_op jit(solution)/shard_map/hand_over/pallas_call | solution.py:848
